TPU v7x, 512 devices: a whole 4x8x8 slice. The times are simulated.
512 devices in a mesh: pts: 64 (over y_lo, z, core), cen: 8 (over x, y_hi).
Axes of the slice: x: 4, y: 8 (y_hi: 2, y_lo: 4; y = y_hi * 4 + y_lo), z: 8, core: 2. Of those that a mesh axis runs over, the one named last changes fastest.
Arguments:
- points: bfloat16 [16384, 256], P('pts'), may hold values from -64 to 64
- centroids: bfloat16 [65536, 256], P('cen'), may hold values from -10 to 10
Outputs:
- updated: float32 [65536, 256], P(('cen', 'pts'))
- log_norm: float32 [16384], P('pts')
All inputs are finite; a program needn't handle non-finite values.
Results may differ from a plain program's by a relative error of at most 0.0017.
Values may be sent and summed in bfloat16 or wider, within the bound.
No kernel may reach another device: no remote copies, remote signals or barrier semaphores. Data moves between devices by JAX's collectives and lax.ppermute only.
A program may use at most 64 MiB of HBM per device.

v0:
```python
import jax
import jax.numpy as jnp
from jax import lax
from jax.sharding import Mesh
from jax.sharding import PartitionSpec as P

PTS = ("pts_0", "pts_1", "pts_2")
CEN_PTS = ("cen", "pts_0", "pts_1", "pts_2")


inv_temp = 0.0625
prior_count = 1.0


def from_everyone(array, axis):
    copies = jnp.broadcast_to(array, (lax.axis_size(axis), *array.shape))
    return lax.all_to_all(copies, axis, split_axis=0, concat_axis=0, tiled=True)


def gathered_once(array, axis):
    leaves = jax.tree.leaves(array)
    sequence = sorted(range(len(leaves)), key=lambda k: -leaves[k].size)
    width = (1, *leaves[sequence[0]].shape)[-1]
    lines = [
        jnp.pad(leaves[k].reshape(-1), (0, -leaves[k].size % width)).reshape(-1, width)
        for k in sequence
    ]
    both, at, found = (from_everyone(jnp.concatenate(lines), axis), 0, {})
    for k, line in zip(sequence, lines):
        section = both[:, at : at + len(line)].reshape(len(both), -1)
        found[k] = section[:, : leaves[k].size].reshape(-1, *leaves[k].shape)
        at += len(line)
    numbers = iter(range(len(leaves)))
    return jax.tree.map(lambda _: found[next(numbers)], array)


def folded_in_pairs(pieces, combine):
    while len(jax.tree.leaves(pieces)[0]) > 1:
        pieces = jax.vmap(combine)(
            *(jax.tree.map(lambda part: part[side::2], pieces) for side in (0, 1))
        )
    return jax.tree.map(lambda part: part[0], pieces)


def joined_all(array, axis, combine):
    pieces = gathered_once(array, axis)
    return folded_in_pairs(pieces, combine)


def joined_along(tiles, dim):
    tiles = jnp.moveaxis(tiles, 0, dim)
    lengths = tiles.shape
    return tiles.reshape(*lengths[:dim], lengths[dim] * lengths[dim + 1], *lengths[dim + 2 :])


def collect(array, axis, dim):
    tiles = from_everyone(array, axis)
    return joined_along(tiles, dim)


def all_blocks(array, axes, sequence):
    tiles = array
    for k in sequence:
        tiles = lax.all_gather(tiles, axes[k])
    done = sequence[::-1]
    back = [done.index(k) for k in range(len(axes))]
    tiles = tiles.transpose(*back, *range(len(axes), tiles.ndim))
    return tiles.reshape(-1, *array.shape)


def gathered_by_axis(array, axes, sequence, dim):
    return joined_along(all_blocks(array, axes, sequence), dim)


def score_rows(rows, table, table_norms):
    products = lax.dot_general(
        rows, table, (((1,), (1,)), ((), ())), preferred_element_type=jnp.float32
    )
    return (2.0 * products - table_norms[None, :]) * inv_temp


def body(points, centroids):
    group_size = lax.axis_size(PTS)
    group_index = lax.axis_index(PTS)
    center_norms = jnp.sum(jnp.square(centroids.astype(jnp.float32)), axis=1)
    logits = score_rows(points, centroids, center_norms)
    local_peak = jnp.max(logits, axis=1)
    local_total = jnp.sum(jnp.exp(logits - local_peak[:, None]), axis=1)

    def combine(earlier, later):
        peak = jnp.maximum(earlier[0], later[0])
        return (peak, earlier[1] * jnp.exp(earlier[0] - peak) + later[1] * jnp.exp(later[0] - peak))

    row_peak, row_total = joined_all((local_peak, local_total), "cen", combine)
    log_norm = row_peak + jnp.log(row_total)
    owned = centroids.shape[0] // group_size
    own_centers = lax.dynamic_slice_in_dim(centroids, group_index * owned, owned, 0)
    own_norms = lax.dynamic_slice_in_dim(center_norms, group_index * owned, owned, 0)
    every_norm = collect(log_norm, PTS, 0)
    segment = gathered_by_axis(points, PTS, (0, 1, 2), 0)
    again = score_rows(segment, own_centers, own_norms)
    rows_used = jnp.exp(again - every_norm[:, None]).astype(jnp.bfloat16)
    weighted = lax.dot_general(
        rows_used, segment, (((0,), (0,)), ((), ())), preferred_element_type=jnp.float32
    )
    masses = jnp.sum(rows_used.astype(jnp.float32), axis=0)
    weighted, masses = (weighted, masses)
    updated = (own_centers.astype(jnp.float32) + weighted) / (prior_count + masses)[:, None]
    return (updated, log_norm)


def solution(mesh):
    torus = Mesh(
        mesh.devices.reshape(4, 8, 2, mesh.shape["cen"]), ("pts_0", "pts_1", "pts_2", "cen")
    )
    in_specs = (P(PTS, None), P("cen", None))
    out_specs = (P(CEN_PTS, None), P(PTS))
    return jax.shard_map(body, mesh=torus, in_specs=in_specs, out_specs=out_specs, check_vma=False)
```

profile of v0, /device:TPU:1, one launch (start us, length us, event | category | flops | bytes accessed | tf_op | source)
XLA Modules:
  0.0 147.5 jit_solution(3110411796240463174)
XLA Ops:
  7.2 0.0 copy-start.1
  7.2 0.0 all-gather.6.cloned.1.call-start
  7.2 15.4 %all-gather = bf16[1024,256]{1,0:T(8,128)(2,1)} all-gather(bf16[256,256]{1,0:T(8,128)(2,1)} %param.2), channel_id=2, replica_groups=mesh['pts_0'=4,'pts_1'=8,'pts_2'=2,'cen'=8] {'pts_0'}, dimensions={0}, use_global_device_ids=true | all-gather | bytes 655360 | tf_op jit(solution)/shard_map/all_gather | solution.py:64
  22.6 0.0 all-gather.6.cloned.1.call-update
  22.7 0.0 all-gather.8.cloned.1.call-start
  22.7 64.8 %all-gather.6.cloned.1.call-done = bf16[32,256,256]{2,1,0:T(8,128)(2,1)} async-done(((bf16[4,256,256]{2,1,0:T(8,128)(2,1)}), bf16[32,256,256]{2,1,0:T(8,128)(2,1)}) %all-gather.6.cloned.1.call-update) | async-done | bytes 4194320 | tf_op jit(solution)/shard_map/all_gather | solution.py:64
  87.5 0.0 all-gather.8.cloned.1.call-update
  87.5 3.3 %multiply_reduce_fusion = f32[8192]{0:T(1024)S(1)} fusion(bf16[8192,256]{1,0:T(8,128)(2,1)} %param.3), kind=kLoop, calls=%fused_computation.11 | loop fusion | flops 6283264 | bytes 4227072 | tf_op jit(solution)/shard_map/reduce_sum | solution.py:85
  90.8 0.0 copy-done.1
  90.8 3.6 %fusion.13 = (f32[256]{0:T(256)S(1)}, f32[256,8192]{1,0:T(8,128)S(1)}) fusion(f32[8192]{0:T(1024)S(1)} %multiply_reduce_fusion, bf16[256,256]{1,0:T(8,128)(2,1)S(1)} %copy-done.1, bf16[8192,256]{1,0:T(8,128)(2,1)} %param.3), kind=kOutput, calls=%fused_computation.29 | convolution fusion | flops 1082130176 | bytes 12747776 | tf_op jit(solution)/shard_map/dot_general | solution.py:76
  94.4 1.4 exponential_reduce_fusion
  95.8 17.6 %all_to_all.11 = f32[8,2,256]{2,1,0:T(2,128)S(1)} all-to-all(f32[8,2,256]{2,1,0:T(2,128)S(1)} %broadcast_in_dim.4), channel_id=1, replica_groups=mesh['pts_0'=4,'pts_1'=8,'pts_2'=2,'cen'=8] {'cen'}, dimensions={0} | all-to-all | bytes 32768 | tf_op jit(solution)/shard_map/all_to_all | solution.py:17
  113.7 0.0 copy-start.2
  113.7 0.7 broadcast_in_dim.5
  114.4 6.9 %all-to-all-start.1 = ((f32[64,1,256]{2,1,0:T(1,128)}), f32[64,1,256]{2,1,0:T(1,128)S(1)}, u32[]{:S(2)}, u32[]{:S(2)}) async-start(f32[64,1,256]{2,1,0:T(1,128)} %broadcast_in_dim.5), calls=%async_computation.1 | async-start | bytes 131072 | tf_op jit(solution)/shard_map/all_to_all | solution.py:17
  121.3 0.1 dynamic_slice.7
  121.4 0.0 all-gather.8.cloned.1.call-done
  121.4 7.6 %copy.8 = bf16[4,8,2,256,256]{4,3,2,1,0:T(8,128)(2,1)} copy(bf16[4,8,2,256,256]{4,3,0,1,2:T(8,128)(2,1)} %bitcast.21) | data formatting | bytes 16777216 | tf_op jit(solution)/shard_map/transpose | solution.py:67
  129.0 0.0 copy-done.2
  129.0 2.2 %all-to-all-done.1 = f32[64,1,256]{2,1,0:T(1,128)S(1)} async-done(((f32[64,1,256]{2,1,0:T(1,128)}), f32[64,1,256]{2,1,0:T(1,128)S(1)}, u32[]{:S(2)}, u32[]{:S(2)}) %all-to-all-start.1) | async-done | bytes 65568 | tf_op jit(solution)/shard_map/all_to_all | solution.py:17
  131.2 0.0 copy-start
  131.2 6.6 %convert_reduce_fusion = (f32[128]{0:T(128)S(1)}, bf16[128,16384]{1,0:T(8,128)(2,1)S(1)}) fusion(f32[16384]{0:T(1024)S(1)} %bitcast.24, f32[128]{0:T(128)S(1)} %dynamic_slice.7, bf16[16384,256]{1,0:T(8,128)(2,1)} %bitcast.19, bf16[8192,256]{1,0:T(8,128)(2,1)} %param.3, s32[]{:T(128)S(6)} %select_n.4), kind=kOutput, calls=%fused_computation.9 | convolution fusion | flops 1088421760 | bytes 12715012 | tf_op jit(solution)/shard_map/dot_general | solution.py:76
  137.9 0.0 copy-done
  137.9 2.8 %fusion.7 = f32[128,256]{1,0:T(8,128)} fusion(bf16[128,16384]{1,0:T(8,128)(2,1)S(1)} %get-tuple-element.11, bf16[16384,256]{1,0:T(8,128)(2,1)S(1)} %bitcast.20, f32[128]{0:T(128)S(1)} %broadcast_add_fusion, bf16[8192,256]{1,0:T(8,128)(2,1)} %param.3, s32[]{:T(128)S(6)} %select_n.4), kind=kOutput, calls=%fused_computation.13 | convolution fusion | flops 1073840128 | bytes 12780036 | tf_op jit(solution)/shard_map/dot_general | solution.py:103
  (16 shorter events, 0.3 us)
Async XLA Ops:
  7.2 83.7 %copy-start.1 = (bf16[256,256]{1,0:T(8,128)(2,1)S(1)}, bf16[256,256]{1,0:T(8,128)(2,1)}, u32[]{:S(2)}) copy-start(bf16[256,256]{1,0:T(8,128)(2,1)} %param.2) | copy-start | bytes 393220
  7.2 80.3 %all-gather.6.cloned.1.call-start = ((), (), s32[]{:S(2)}) async-start(), calls=%async_computation.2 | async-start | bytes 4718592 | tf_op jit(solution)/shard_map/all_gather | solution.py:64
  22.7 98.8 %all-gather.8.cloned.1.call-start = ((), (), s32[]{:S(2)}) async-start(), calls=%async_computation.3 | async-start | bytes 12582912 | tf_op jit(solution)/shard_map/all_gather | solution.py:64
  113.7 15.3 %copy-start.2 = (f32[1,256]{1,0:T(1,128)}, f32[1,256]{1,0:T(1,128)S(1)}, u32[]{:S(2)}) copy-start(f32[1,256]{1,0:T(1,128)S(1)} %log_add_fusion) | copy-start | bytes 3076
  114.4 16.8 %all-to-all-start.1 = ((f32[64,1,256]{2,1,0:T(1,128)}), f32[64,1,256]{2,1,0:T(1,128)S(1)}, u32[]{:S(2)}, u32[]{:S(2)}) async-start(f32[64,1,256]{2,1,0:T(1,128)} %broadcast_in_dim.5), calls=%async_computation.1 | async-start | bytes 131072 | tf_op jit(solution)/shard_map/all_to_all | solution.py:17
  131.2 6.6 %copy-start = (bf16[4,8,2,256,256]{4,3,2,1,0:T(8,128)(2,1)S(1)}, bf16[4,8,2,256,256]{4,3,2,1,0:T(8,128)(2,1)}, u32[]{:S(2)}) copy-start(bf16[4,8,2,256,256]{4,3,2,1,0:T(8,128)(2,1)} %copy.8) | copy-start | bytes 25165828
Sparse Core Ops, SparseCore 0:
  22.8 64.6 all-gather.5
  89.5 27.5 all-gather.7
where the time goes:
time: 148 us; the launch traced here: 147 us
  waiting for transfers between devices  67 us (45%)
  blocking collectives  33.1 us (22%)
  between operations  14.1 us (10%)
  matrix products  12.9 us (9%)
  local copies, waits for them, and re-layouts  8.55 us (6%)
  starting transfers between devices  6.99 us (5%)
  other arithmetic  4.77 us (3%)
    all_gather x2, waiting for transfers between devices, all_blocks(): tiles = lax.all_gather(tiles, axes[k])  64.8 us
    all_to_all x1, blocking collectives, from_everyone(): return lax.all_to_all(copies, axis, split_axis=0, concat_axis=0, tiled=True)  17.6 us
    all_gather x1, blocking collectives, all_blocks(): tiles = lax.all_gather(tiles, axes[k])  15.4 us
    dot_general x2, matrix products, score_rows(): lax.dot_general(rows, table, (((1,), (1,)), ((), ())), preferred_element_...  10.2 us
    transpose x1, local copies, waits for them, and re-layouts, all_blocks(): tiles = tiles.transpose(*back, *range(len(axes), tiles.ndim))  7.59 us
    all_to_all x1, starting transfers between devices, from_everyone(): return lax.all_to_all(copies, axis, split_axis=0, concat_axis=0, tiled=True)  6.91 us
    reduce_sum x1, other arithmetic, body(): center_norms = jnp.sum(jnp.square(centroids.astype(jnp.float32)), axis=1)  3.34 us
  transfers between devices with their start and end apart: 3, of which 2 were waited for; matrix products, arithmetic and copies ran while one was open for 11% of the time, Pallas kernels for 0%

commit v1 on v0

v1 whole, which is shorter than its diff:
```python
import jax
import jax.numpy as jnp
from jax import lax
from jax.experimental import pallas as pl
from jax.experimental.pallas import tpu as pltpu
from jax.sharding import Mesh
from jax.sharding import PartitionSpec as P

AXES = ("ya", "yb", "za", "zb", "co")
GATHER = ("yb", "zb", "co")
REDUCE = ("ya", "za")
CEN = "cen"
MIB = 1 << 20
inv_temp = 0.0625


def scores(table, rows):
    wide = table.astype(jnp.float32)
    norms = jnp.sum(wide * wide, axis=1, keepdims=True)
    products = lax.dot_general(
        table, rows, (((1,), (1,)), ((), ())), preferred_element_type=jnp.float32
    )
    return (2.0 * products - norms) * inv_temp


def first_kernel(table, rows, stats, peak, total):
    step = pl.program_id(0)

    @pl.when(step == 0)
    def _():
        peak[...] = jnp.full_like(peak, -jnp.inf)
        total[...] = jnp.zeros_like(total)

    logits = scores(table[...], rows[...])
    top = jnp.maximum(peak[...], jnp.max(logits, axis=0, keepdims=True))
    total[...] = total[...] * jnp.exp(peak[...] - top) + jnp.sum(
        jnp.exp(logits - top), axis=0, keepdims=True
    )
    peak[...] = top

    @pl.when(step == pl.num_programs(0) - 1)
    def _():
        stats[0:1, :] = peak[...]
        stats[1:2, :] = total[...]


def first_pass(points, centroids):
    n, d = points.shape
    k = centroids.shape[0]
    block = 1024
    return pl.pallas_call(
        first_kernel,
        grid=(k // block,),
        in_specs=[
            pl.BlockSpec((block, d), lambda i: (i, 0)),
            pl.BlockSpec((n, d), lambda i: (0, 0)),
        ],
        out_specs=pl.BlockSpec((2, n), lambda i: (0, 0)),
        out_shape=jax.ShapeDtypeStruct((2, n), jnp.float32),
        scratch_shapes=[pltpu.VMEM((1, n), jnp.float32)] * 2,
        compiler_params=pltpu.CompilerParams(vmem_limit_bytes=60 * MIB),
        cost_estimate=pl.CostEstimate(
            flops=2 * n * k * d, bytes_accessed=2 * k * d, transcendentals=n * k
        ),
        name="first_pass",
    )(centroids, points)


def second_kernel(place, stats, table, near, across, up, far, sums, log_norms):
    yb, zb = place[1], place[3]

    @pl.when(pl.program_id(0) == 0)
    def _():
        cen = stats.shape[0]
        peak = stats[0, :, 0, :]
        for c in range(1, cen):
            peak = jnp.maximum(peak, stats[c, :, 0, :])
        total = stats[0, :, 1, :] * jnp.exp(stats[0, :, 0, :] - peak)
        for c in range(1, cen):
            total = total + stats[c, :, 1, :] * jnp.exp(stats[c, :, 0, :] - peak)
        log_norms[...] = peak + jnp.log(total)

    _, owned, d = table.shape
    product = jnp.zeros((owned, d), jnp.float32)
    mass = jnp.zeros((8, owned), jnp.float32)
    pairs = ((near, yb, zb), (across, yb, 1 - zb), (up, 1 - yb, zb), (far, 1 - yb, 1 - zb))
    for rows, y, z in pairs:
        for c in range(2):
            logits = scores(table[0], rows[c])
            shift = log_norms[pl.ds((y * 2 + z) * 2 + c, 1), :]
            shares = jnp.exp(logits - shift).astype(jnp.bfloat16)
            product += lax.dot_general(
                shares, rows[c], (((1,), (0,)), ((), ())), preferred_element_type=jnp.float32
            )
            mass += lax.dot_general(
                jnp.ones((8, shares.shape[1]), jnp.bfloat16),
                shares,
                (((1,), (1,)), ((), ())),
                preferred_element_type=jnp.float32,
            )
    sums[0, :owned, :] = product
    sums[0, owned:, :] = jnp.concatenate([mass, jnp.zeros((8, d - owned), jnp.float32)], axis=1)


def second_pass(place, stats, table, blocks):
    reduced, owned, d = table.shape
    g, n = stats.shape[1], stats.shape[3]
    k = owned * reduced
    whole = pl.BlockSpec(blocks[0].shape, lambda i, place: (0, 0, 0))
    return pl.pallas_call(
        second_kernel,
        grid_spec=pltpu.PrefetchScalarGridSpec(
            num_scalar_prefetch=1,
            grid=(reduced,),
            in_specs=[
                pl.BlockSpec(stats.shape, lambda i, place: (0, 0, 0, 0)),
                pl.BlockSpec((1, owned, d), lambda i, place: (i, 0, 0)),
                *[whole] * 4,
            ],
            out_specs=[
                pl.BlockSpec((1, owned + 8, d), lambda i, place: (i, 0, 0)),
                pl.BlockSpec((g, n), lambda i, place: (0, 0)),
            ],
        ),
        out_shape=[
            jax.ShapeDtypeStruct((reduced, owned + 8, d), jnp.float32),
            jax.ShapeDtypeStruct((g, n), jnp.float32),
        ],
        compiler_params=pltpu.CompilerParams(vmem_limit_bytes=24 * MIB),
        cost_estimate=pl.CostEstimate(
            flops=4 * g * n * k * d, bytes_accessed=4 * k * d, transcendentals=g * n * k
        ),
        name="second_pass",
    )(place, stats, table, *blocks)


def last_kernel(place, parts, table, updated):
    owned = table.shape[1]
    total = parts[0]
    for r in range(1, parts.shape[0]):
        total = total + parts[r]
    mass = jnp.broadcast_to(total[owned : owned + 1, :owned], (owned, owned)).T
    for at in range(0, updated.shape[1], owned):
        here = slice(at, at + owned)
        updated[:, here] = (table[0, :, here].astype(jnp.float32) + total[:owned, here]) / (
            1.0 + mass
        )


def last_pass(place, parts, table):
    reduced, owned, d = table.shape

    def own(i, place):
        return (place[0] * (reduced // 2) + place[2], 0, 0)

    return pl.pallas_call(
        last_kernel,
        grid_spec=pltpu.PrefetchScalarGridSpec(
            num_scalar_prefetch=1,
            grid=(1,),
            in_specs=[
                pl.BlockSpec(parts.shape, lambda i, place: (0, 0, 0)),
                pl.BlockSpec((1, owned, d), own),
            ],
            out_specs=pl.BlockSpec((owned, d), lambda i, place: (0, 0)),
        ),
        out_shape=jax.ShapeDtypeStruct((owned, d), jnp.float32),
        compiler_params=pltpu.CompilerParams(vmem_limit_bytes=24 * MIB),
        name="last_pass",
    )(place, parts, table)


def body(points, centroids):
    n, d = points.shape
    cen = lax.axis_size(CEN)
    gathered = lax.axis_size(GATHER)
    reduced = lax.axis_size(REDUCE)
    owned = centroids.shape[0] // (gathered * reduced)
    place = jnp.stack([lax.axis_index(a) for a in AXES]).astype(jnp.int32)
    swap = [(0, 1), (1, 0)]

    near = lax.all_gather(points, "co")
    across = lax.ppermute(near, "zb", swap)
    up = lax.ppermute(near, "yb", swap)
    stats = first_pass(points, centroids)
    across, stats = lax.optimization_barrier((across, stats))
    far = lax.ppermute(across, "yb", swap)
    copies = jnp.broadcast_to(stats, (cen * gathered, 2, n))
    every = lax.all_to_all(copies, (CEN, *GATHER), 0, 0, tiled=True)
    every = every.reshape(cen, gathered, 2, n)
    sizes = [lax.axis_size(a) for a in AXES]
    at = (0, place[1], 0, place[3], place[4], 0, 0)
    cut = (sizes[0], 1, sizes[2], 1, 1, owned, d)
    table = lax.dynamic_slice(centroids.reshape(*sizes, owned, d), at, cut)
    table = table.reshape(reduced, owned, d)
    parts, log_norms = second_pass(place, every, table, (near, across, up, far))
    parts = lax.all_to_all(parts, REDUCE, 0, 0, tiled=True)
    updated = last_pass(place, parts, table)
    log_norm = lax.dynamic_slice_in_dim(log_norms, lax.axis_index(GATHER), 1, 0)[0]
    return updated, log_norm


def solution(mesh):
    shape = (2, 2, 4, 2, 2, mesh.shape["cen"])
    torus = Mesh(mesh.devices.reshape(shape), (*AXES, CEN))
    in_specs = (P(AXES, None), P(CEN, None))
    out_specs = (P((CEN, *AXES), None), P(AXES))
    return jax.shard_map(body, mesh=torus, in_specs=in_specs, out_specs=out_specs, check_vma=False)
```

time: 148 us -> 105 us (0.71)
  the two profiles are of different devices: /device:TPU:1 before, /device:TPU:24 now
where the time goes in v1:
time: 105 us
  waiting for transfers between devices  43.5 us (41%)
  starting transfers between devices  31.1 us (30%)
  Pallas kernels  24.1 us (23%)
  local copies, waits for them, and re-layouts  3.09 us (3%)
  blocking collectives  2.21 us (2%)
    all_to_all x1, waiting for transfers between devices, body(): parts = lax.all_to_all(parts, REDUCE, 0, 0, tiled=True)  33.9 us
    pallas_call x1, Pallas kernels, second_pass(): pl.pallas_call(second_kernel, grid_spec=pltpu.PrefetchScalarGridSpec(num_...  15 us
    all_to_all x1, starting transfers between devices, body(): parts = lax.all_to_all(parts, REDUCE, 0, 0, tiled=True)  12.2 us
    all_to_all x1, waiting for transfers between devices, body(): every = lax.all_to_all(copies, (CEN, *GATHER), 0, 0, tiled=True)  9.52 us
    all_to_all x1, starting transfers between devices, body(): every = lax.all_to_all(copies, (CEN, *GATHER), 0, 0, tiled=True)  8.78 us
    pallas_call x1, Pallas kernels, first_pass(): pl.pallas_call(first_kernel, grid=(k // block,), in_specs=[pl.BlockSpec((...  7.75 us
    ppermute x1, starting transfers between devices, body(): across = lax.ppermute(near, 'zb', swap)  4.27 us
    ppermute x1, starting transfers between devices, body(): far = lax.ppermute(across, 'yb', swap)  3.46 us
  transfers between devices with their start and end apart: 5, of which 2 were waited for; matrix products, arithmetic and copies ran while one was open for 3% of the time, Pallas kernels for 7%

profile of v1, /device:TPU:24, one launch (start us, length us, event | category | flops | bytes accessed | tf_op | source)
XLA Modules:
  0.0 104.6 jit_solution(627637567120553553)
XLA Ops:
  0.6 2.2 %all-gather = bf16[512,256]{1,0:T(8,128)(2,1)S(1)} all-gather(bf16[256,256]{1,0:T(8,128)(2,1)} %rows.1), channel_id=2, replica_groups=mesh['ya'=2,'yb'=2,'za'=4,'zb'=2,'co'=2,'cen'=8] {'co'}, dimensions={0}, use_global_device_ids=true | all-gather | bytes 393216 | tf_op jit(solution)/shard_map/all_gather | solution.py:182
  2.8 4.3 %collective-permute-start = (bf16[2,256,256]{2,1,0:T(8,128)(2,1)S(1)}, bf16[2,256,256]{2,1,0:T(8,128)(2,1)S(1)}, u32[]{:S(2)}, u32[]{:S(2)}) collective-permute-start(bf16[2,256,256]{2,1,0:T(8,128)(2,1)S(1)} %bitcast.14), channel_id=1, source_target_pairs={{0,16},{16,0},{1,17},{17,1},{2,18},{18,2},{3,19},{19,3},{4,20},{20... | collective-permute-start | bytes 786440 | tf_op jit(solution)/shard_map/ppermute | solution.py:183
  7.1 2.4 %collective-permute-start.1 = (bf16[2,256,256]{2,1,0:T(8,128)(2,1)S(1)}, bf16[2,256,256]{2,1,0:T(8,128)(2,1)S(1)}, u32[]{:S(2)}, u32[]{:S(2)}) collective-permute-start(bf16[2,256,256]{2,1,0:T(8,128)(2,1)S(1)} %bitcast.15), channel_id=1, source_target_pairs={{0,128},{128,0},{1,129},{129,1},{2,130},{130,2},{3,131},{131,3},{4... | collective-permute-start | bytes 786440 | tf_op jit(solution)/shard_map/ppermute | solution.py:184
  9.5 7.7 %first_pass.1 = f32[2,256]{1,0:T(2,128)} custom-call(bf16[8192,256]{1,0:T(8,128)(2,1)} %table.1, bf16[256,256]{1,0:T(8,128)(2,1)} %rows.1), custom_call_target="tpu_custom_call" | custom-call | flops 1073741824 | bytes 4194304 | tf_op jit(solution)/shard_map/first_pass/pallas_call | solution.py:51
  17.2 0.0 collective-permute-done.across
  17.2 3.5 %collective-permute-start.2 = (bf16[2,256,256]{2,1,0:T(8,128)(2,1)S(1)}, bf16[2,256,256]{2,1,0:T(8,128)(2,1)S(1)}, u32[]{:S(2)}, u32[]{:S(2)}) collective-permute-start(bf16[2,256,256]{2,1,0:T(8,128)(2,1)S(1)} %collective-permute-done.across), channel_id=1, source_target_pairs={{0,128},{128,0},{1,129},{129,1},{2,130},{130,2},{3,131},{131,3},{4... | collective-permute-start | bytes 786440 | tf_op jit(solution)/shard_map/ppermute | solution.py:187
  20.7 1.4 %broadcast_in_dim.3 = f32[64,2,256]{2,1,0:T(2,128)} broadcast(f32[2,256]{1,0:T(2,128)} %first_pass.1), dimensions={1,2} | broadcast | bytes 133120 | tf_op jit(solution)/shard_map/broadcast_in_dim | solution.py:188
  22.1 8.8 %all-to-all-start = ((f32[64,2,256]{2,1,0:T(2,128)}), f32[64,2,256]{2,1,0:T(2,128)S(1)}, u32[]{:S(2)}, u32[]{:S(2)}) async-start(f32[64,2,256]{2,1,0:T(2,128)} %broadcast_in_dim.3), calls=%async_computation | async-start | bytes 262144 | tf_op jit(solution)/shard_map/all_to_all | solution.py:189
  30.9 0.1 stack.23.place
  30.9 1.1 %constant_dynamic-slice_fusion.1 = bf16[2,1,4,1,1,128,256]{6,5,4,3,2,1,0:T(8,128)(2,1)S(1)} fusion(bf16[2,2,4,2,2,128,256]{6,5,4,3,2,1,0:T(8,128)(2,1)} %bitcast.18, s32[]{:T(128)S(6)} %select_n.12, s32[]{:T(128)S(6)} %select_n.13, s32[]{:T(128)S(6)} %select_n.14), kind=kLoop, calls=%fused_computation.1 | loop fusion | bytes 1048588 | tf_op jit(solution)/shard_map/dynamic_slice | solution.py:194
  32.0 0.0 collective-permute-done.1.up
  32.0 9.5 %all-to-all-done = f32[64,2,256]{2,1,0:T(2,128)S(1)} async-done(((f32[64,2,256]{2,1,0:T(2,128)}), f32[64,2,256]{2,1,0:T(2,128)S(1)}, u32[]{:S(2)}, u32[]{:S(2)}) %all-to-all-start) | async-done | bytes 131104 | tf_op jit(solution)/shard_map/all_to_all | solution.py:189
  41.6 0.0 collective-permute-done.2.far
  41.6 15.0 %second_pass.1 = (f32[8,136,256]{2,1,0:T(8,128)}, f32[8,256]{1,0:T(8,128)S(1)}) custom-call(s32[5]{0:T(128)S(1)} %stack.23.place, f32[8,8,2,256]{3,2,1,0:T(2,128)S(1)} %bitcast.17, bf16[8,128,256]{2,1,0:T(8,128)(2,1)S(1)} %bitcast.12, bf16[2,256,256]{2,1,0:T(8,128)(2,1)S(1)} %bitcast.16, bf16[2,256,256]{2,1,0:T(8,128)(2,1)S(1)} %collective-permute-done.across, ...), custom_call_target="tpu_custom_call" | custom-call | flops 2147483648 | bytes 1048576 | tf_op jit(solution)/shard_map/second_pass/pallas_call | solution.py:110
  56.6 12.2 %all-to-all-start.1 = ((f32[8,136,256]{2,1,0:T(8,128)}), f32[8,136,256]{2,1,0:T(8,128)S(1)}, u32[]{:S(2)}, u32[]{:S(2)}) async-start(f32[8,136,256]{2,1,0:T(8,128)} %get-tuple-element.8), calls=%async_computation.1 | async-start | bytes 2228224 | tf_op jit(solution)/shard_map/all_to_all | solution.py:197
  68.8 0.6 constant_dynamic-slice_fusion
  69.4 33.9 %all-to-all-done.1.parts = f32[8,136,256]{2,1,0:T(8,128)S(1)} async-done(((f32[8,136,256]{2,1,0:T(8,128)}), f32[8,136,256]{2,1,0:T(8,128)S(1)}, u32[]{:S(2)}, u32[]{:S(2)}) %all-to-all-start.1) | async-done | bytes 1114144 | tf_op jit(solution)/shard_map/all_to_all | solution.py:197
  103.3 1.3 %last_pass.1 = f32[128,256]{1,0:T(8,128)} custom-call(s32[5]{0:T(128)S(1)} %stack.23.place, f32[8,136,256]{2,1,0:T(8,128)S(1)} %all-to-all-done.1.parts, bf16[8,128,256]{2,1,0:T(8,128)(2,1)S(1)} %bitcast.13), custom_call_target="tpu_custom_call" | custom-call | tf_op jit(solution)/shard_map/last_pass/pallas_call | solution.py:156
Async XLA Ops:
  2.8 14.4 %collective-permute-start = (bf16[2,256,256]{2,1,0:T(8,128)(2,1)S(1)}, bf16[2,256,256]{2,1,0:T(8,128)(2,1)S(1)}, u32[]{:S(2)}, u32[]{:S(2)}) collective-permute-start(bf16[2,256,256]{2,1,0:T(8,128)(2,1)S(1)} %bitcast.14), channel_id=1, source_target_pairs={{0,16},{16,0},{1,17},{17,1},{2,18},{18,2},{3,19},{19,3},{4,20},{20... | collective-permute-start | bytes 786440 | tf_op jit(solution)/shard_map/ppermute | solution.py:183
  7.1 24.9 %collective-permute-start.1 = (bf16[2,256,256]{2,1,0:T(8,128)(2,1)S(1)}, bf16[2,256,256]{2,1,0:T(8,128)(2,1)S(1)}, u32[]{:S(2)}, u32[]{:S(2)}) collective-permute-start(bf16[2,256,256]{2,1,0:T(8,128)(2,1)S(1)} %bitcast.15), channel_id=1, source_target_pairs={{0,128},{128,0},{1,129},{129,1},{2,130},{130,2},{3,131},{131,3},{4... | collective-permute-start | bytes 786440 | tf_op jit(solution)/shard_map/ppermute | solution.py:184
  17.2 24.3 %collective-permute-start.2 = (bf16[2,256,256]{2,1,0:T(8,128)(2,1)S(1)}, bf16[2,256,256]{2,1,0:T(8,128)(2,1)S(1)}, u32[]{:S(2)}, u32[]{:S(2)}) collective-permute-start(bf16[2,256,256]{2,1,0:T(8,128)(2,1)S(1)} %collective-permute-done.across), channel_id=1, source_target_pairs={{0,128},{128,0},{1,129},{129,1},{2,130},{130,2},{3,131},{131,3},{4... | collective-permute-start | bytes 786440 | tf_op jit(solution)/shard_map/ppermute | solution.py:187
  22.1 19.5 %all-to-all-start = ((f32[64,2,256]{2,1,0:T(2,128)}), f32[64,2,256]{2,1,0:T(2,128)S(1)}, u32[]{:S(2)}, u32[]{:S(2)}) async-start(f32[64,2,256]{2,1,0:T(2,128)} %broadcast_in_dim.3), calls=%async_computation | async-start | bytes 262144 | tf_op jit(solution)/shard_map/all_to_all | solution.py:189
  56.6 46.7 %all-to-all-start.1 = ((f32[8,136,256]{2,1,0:T(8,128)}), f32[8,136,256]{2,1,0:T(8,128)S(1)}, u32[]{:S(2)}, u32[]{:S(2)}) async-start(f32[8,136,256]{2,1,0:T(8,128)} %get-tuple-element.8), calls=%async_computation.1 | async-start | bytes 2228224 | tf_op jit(solution)/shard_map/all_to_all | solution.py:197

commit v2 on v1

v2 whole, which is shorter than its diff:
```python
import jax
import jax.numpy as jnp
from jax import lax
from jax.experimental import pallas as pl
from jax.experimental.pallas import tpu as pltpu
from jax.sharding import Mesh
from jax.sharding import PartitionSpec as P

AXES = ("ya", "yb", "za", "zb", "co")
GATHER = ("yb", "zb", "co")
REDUCE = ("ya", "za")
CEN = "cen"
MIB = 1 << 20
CHUNK = 1024
inv_temp = 0.0625
SPAN, FLOOR = 240.0, 120.0


def squares(table):
    wide = table.astype(jnp.float32)
    return jnp.sum(wide * wide, axis=1, keepdims=True) * inv_temp


def products(table, rows):
    return lax.dot_general(
        table,
        rows * jnp.bfloat16(2.0 * inv_temp),
        (((1,), (1,)), ((), ())),
        preferred_element_type=jnp.float32,
    )


def first_kernel(centroids, rows, stats, table, arrived):
    chunks = table.shape[0] // CHUNK

    def copy(i):
        here = pl.ds(i * CHUNK, CHUNK)
        return pltpu.make_async_copy(centroids.at[here], table.at[here], arrived.at[i])

    for i in range(chunks):
        copy(i).start()

    def step(i, carry):
        peak, total = carry
        copy(i).wait()
        block = table[pl.ds(pl.multiple_of(i * CHUNK, CHUNK), CHUNK), :]
        logits = products(block, rows[...]) - squares(block)
        top = jnp.maximum(peak, jnp.max(logits, axis=0, keepdims=True))
        total = total * jnp.exp(peak - top) + jnp.sum(jnp.exp(logits - top), axis=0, keepdims=True)
        return top, total

    n = rows.shape[0]
    start = (jnp.full((1, n), -jnp.inf, jnp.float32), jnp.zeros((1, n), jnp.float32))
    peak, total = lax.fori_loop(0, chunks, step, start)
    stats[0:1, :] = peak
    stats[1:2, :] = total


def first_pass(points, centroids):
    n, d = points.shape
    k = centroids.shape[0]
    return pl.pallas_call(
        first_kernel,
        in_specs=[
            pl.BlockSpec(memory_space=pltpu.HBM),
            pl.BlockSpec(memory_space=pltpu.VMEM),
        ],
        out_specs=pl.BlockSpec(memory_space=pltpu.VMEM),
        out_shape=jax.ShapeDtypeStruct((2, n), jnp.float32),
        scratch_shapes=[
            pltpu.VMEM((k, d), centroids.dtype),
            pltpu.SemaphoreType.DMA((k // CHUNK,)),
        ],
        compiler_params=pltpu.CompilerParams(vmem_limit_bytes=20 * MIB),
        cost_estimate=pl.CostEstimate(
            flops=2 * n * k * d, bytes_accessed=2 * k * d, transcendentals=n * k
        ),
        name="first_pass",
    )(pltpu.with_memory_space_constraint(centroids, pltpu.HBM), points)


def second_kernel(stats, table, near, across, up, far, parts, own_norm, log_norms, sums, masses):
    yb, zb, co = (lax.axis_index(a) for a in GATHER)

    cen = stats.shape[0]
    peak = stats[0, :, 0, :]
    for c in range(1, cen):
        peak = jnp.maximum(peak, stats[c, :, 0, :])
    total = stats[0, :, 1, :] * jnp.exp(stats[0, :, 0, :] - peak)
    for c in range(1, cen):
        total = total + stats[c, :, 1, :] * jnp.exp(stats[c, :, 0, :] - peak)
    log_norms[...] = peak + jnp.log(total)
    own_norm[...] = log_norms[pl.ds((yb * 2 + zb) * 2 + co, 1), :]

    norms = squares(table[...])
    pairs = ((near, yb, zb), (across, yb, 1 - zb), (up, 1 - yb, zb), (far, 1 - yb, 1 - zb))
    for at, (rows, y, z) in enumerate(pairs):
        for c in range(2):
            shift = log_norms[pl.ds((y * 2 + z) * 2 + c, 1), :]
            logits = products(table[...], rows[c]) - norms
            shares = jnp.exp(logits - shift).astype(jnp.bfloat16)
            product = lax.dot_general(
                shares, rows[c], (((1,), (0,)), ((), ())), preferred_element_type=jnp.float32
            )
            wide = shares.astype(jnp.float32)
            mass = wide[:, :128] + wide[:, 128:]
            if at == 0 and c == 0:
                sums[...] = product
                masses[...] = mass
            else:
                sums[...] += product
                masses[...] += mass

    owned, d = parts.shape[1] - 16, parts.shape[2]
    line = lax.broadcasted_iota(jnp.int32, (16, d), 0)
    for r in range(parts.shape[0]):
        here = slice(r * owned, (r + 1) * owned)
        mass = masses[here, :]
        mean = sums[here, :] / (1.0 + jnp.sum(mass, axis=1, keepdims=True))
        size = jnp.abs(mean)
        scale = jnp.maximum(jnp.max(size, axis=0, keepdims=True) * 1.01, 1e-30)
        scale = scale.astype(jnp.bfloat16).astype(jnp.float32)
        code = jnp.exp2(size * (SPAN / scale) - FLOOR)
        parts[r, :owned, :] = jnp.where(mean < 0.0, -code, code).astype(jnp.bfloat16)
        mass = jnp.sum(mass.T, axis=0, keepdims=True)
        high = mass.astype(jnp.bfloat16).astype(jnp.float32)
        mid = (mass - high).astype(jnp.bfloat16).astype(jnp.float32)
        low = mass - high - mid
        upper = jnp.concatenate([high, mid], axis=1)
        lower = jnp.concatenate([low, jnp.zeros_like(low)], axis=1)
        tail = jnp.where(line == 0, scale, jnp.where(line == 1, upper, lower))
        parts[r, owned:, :] = tail.astype(jnp.bfloat16)


def second_pass(stats, table, blocks):
    reduced, owned, d = table.shape
    g, n = stats.shape[1], stats.shape[3]
    k = owned * reduced
    return pl.pallas_call(
        second_kernel,
        in_specs=[pl.BlockSpec(memory_space=pltpu.VMEM)] * 6,
        out_specs=[pl.BlockSpec(memory_space=pltpu.VMEM)] * 2,
        out_shape=[
            jax.ShapeDtypeStruct((reduced, owned + 16, d), jnp.bfloat16),
            jax.ShapeDtypeStruct((1, n), jnp.float32),
        ],
        scratch_shapes=[
            pltpu.VMEM((g, n), jnp.float32),
            pltpu.VMEM((k, d), jnp.float32),
            pltpu.VMEM((k, 128), jnp.float32),
        ],
        compiler_params=pltpu.CompilerParams(vmem_limit_bytes=24 * MIB),
        cost_estimate=pl.CostEstimate(
            flops=4 * g * n * k * d, bytes_accessed=4 * k * d, transcendentals=g * n * k
        ),
        name="second_pass",
    )(stats, table.reshape(k, d), *blocks)


def last_kernel(parts, table, updated):
    owned = updated.shape[0]
    own = table[lax.axis_index("ya") * lax.axis_size("za") + lax.axis_index("za")]
    sums = own.astype(jnp.float32)
    masses = jnp.ones((owned, owned), jnp.float32)
    for r in range(parts.shape[0]):
        tail = parts[r, owned:, :].astype(jnp.float32)
        mass = tail[1:2, :owned] + tail[1:2, owned:] + tail[2:3, :owned]
        mass = jnp.broadcast_to(mass, (owned, owned)).T
        code = parts[r, :owned, :].astype(jnp.float32)
        size = (jnp.log2(jnp.abs(code)) + FLOOR) * (tail[0:1, :] / SPAN)
        mean = jnp.where(code < 0.0, -size, size)
        weight = 1.0 + mass
        sums = sums + mean * jnp.concatenate([weight, weight], axis=1)
        masses = masses + mass
    updated[...] = sums / jnp.concatenate([masses, masses], axis=1)


def last_pass(parts, table):
    reduced, owned, d = table.shape
    return pl.pallas_call(
        last_kernel,
        in_specs=[pl.BlockSpec(memory_space=pltpu.VMEM)] * 2,
        out_specs=pl.BlockSpec(memory_space=pltpu.VMEM),
        out_shape=jax.ShapeDtypeStruct((owned, d), jnp.float32),
        compiler_params=pltpu.CompilerParams(vmem_limit_bytes=16 * MIB),
        name="last_pass",
    )(parts, table)


def body(points, centroids):
    n, d = points.shape
    cen = lax.axis_size(CEN)
    gathered = lax.axis_size(GATHER)
    reduced = lax.axis_size(REDUCE)
    owned = centroids.shape[0] // (gathered * reduced)
    swap = [(0, 1), (1, 0)]

    near = lax.all_gather(points, "co")
    across = lax.ppermute(near, "zb", swap)
    up = lax.ppermute(near, "yb", swap)
    stats = first_pass(points, centroids)
    copies = jnp.broadcast_to(stats, (cen * gathered, 2, n))
    across, copies = lax.optimization_barrier((across, copies))
    far = lax.ppermute(across, "yb", swap)
    every = lax.all_to_all(copies, (CEN, *GATHER), 0, 0, tiled=True)
    every = every.reshape(cen, gathered, 2, n)
    sizes = [lax.axis_size(a) for a in AXES]
    at = (0, lax.axis_index("yb"), 0, lax.axis_index("zb"), lax.axis_index("co"), 0, 0)
    cut = (sizes[0], 1, sizes[2], 1, 1, owned, d)
    table = lax.dynamic_slice(centroids.reshape(*sizes, owned, d), at, cut)
    table = table.reshape(reduced, owned, d)
    parts, log_norm = second_pass(every, table, (near, across, up, far))
    parts = lax.all_to_all(parts, REDUCE, 0, 0, tiled=True)
    return last_pass(parts, table), log_norm[0]


def solution(mesh):
    shape = (2, 2, 4, 2, 2, mesh.shape["cen"])
    torus = Mesh(mesh.devices.reshape(shape), (*AXES, CEN))
    in_specs = (P(AXES, None), P(CEN, None))
    out_specs = (P((CEN, *AXES), None), P(AXES))
    return jax.shard_map(body, mesh=torus, in_specs=in_specs, out_specs=out_specs, check_vma=False)
```

time: 105 us -> 76.5 us (0.73)
  the two profiles are of different devices: /device:TPU:24 before, /device:TPU:1 now
where the time goes in v2:
time: 76.5 us; the launch traced here: 76 us
  blocking collectives  37.2 us (49%)
  starting transfers between devices  15.2 us (20%)
  Pallas kernels  10.5 us (14%)
  waiting for transfers between devices  9.7 us (13%)
  local copies, waits for them, and re-layouts  2.68 us (4%)
    all_to_all x1, blocking collectives, body(): parts = lax.all_to_all(parts, REDUCE, 0, 0, tiled=True)  28.5 us
    all_to_all x1, waiting for transfers between devices, body(): every = lax.all_to_all(copies, (CEN, *GATHER), 0, 0, tiled=True)  9.69 us
    all_gather x1, blocking collectives, body(): near = lax.all_gather(points, 'co')  8.72 us
    all_to_all x1, starting transfers between devices, body(): every = lax.all_to_all(copies, (CEN, *GATHER), 0, 0, tiled=True)  8.03 us
    pallas_call x1, Pallas kernels, first_pass(): pl.pallas_call(first_kernel, in_specs=[pl.BlockSpec(memory_space=pltpu.HB...  5.8 us
    pallas_call x1, Pallas kernels, second_pass(): pl.pallas_call(second_kernel, in_specs=[pl.BlockSpec(memory_space=pltpu.V...  3.65 us
    ppermute x1, starting transfers between devices, body(): far = lax.ppermute(across, 'yb', swap)  3.35 us
    ppermute x1, starting transfers between devices, body(): up = lax.ppermute(near, 'yb', swap)  1.92 us
  transfers between devices with their start and end apart: 4, of which 1 were waited for; matrix products, arithmetic and copies ran while one was open for 2% of the time, Pallas kernels for 8%

profile of v2, /device:TPU:1, one launch (start us, length us, event | category | flops | bytes accessed | tf_op | source)
XLA Modules:
  0.0 76.0 jit_solution(15324483667590644226)
XLA Ops:
  0.6 8.7 %all-gather = bf16[512,256]{1,0:T(8,128)(2,1)S(1)} all-gather(bf16[256,256]{1,0:T(8,128)(2,1)} %rows.1), channel_id=2, replica_groups=mesh['ya'=2,'yb'=2,'za'=4,'zb'=2,'co'=2,'cen'=8] {'co'}, dimensions={0}, use_global_device_ids=true | all-gather | bytes 393216 | tf_op jit(solution)/shard_map/all_gather | solution.py:198
  9.4 1.9 %collective-permute-start = (bf16[2,256,256]{2,1,0:T(8,128)(2,1)S(1)}, bf16[2,256,256]{2,1,0:T(8,128)(2,1)S(1)}, u32[]{:S(2)}, u32[]{:S(2)}) collective-permute-start(bf16[2,256,256]{2,1,0:T(8,128)(2,1)S(1)} %bitcast.11), channel_id=1, source_target_pairs={{0,16},{16,0},{1,17},{17,1},{2,18},{18,2},{3,19},{19,3},{4,20},{20... | collective-permute-start | bytes 786440 | tf_op jit(solution)/shard_map/ppermute | solution.py:199
  11.3 1.9 %collective-permute-start.1 = (bf16[2,256,256]{2,1,0:T(8,128)(2,1)S(1)}, bf16[2,256,256]{2,1,0:T(8,128)(2,1)S(1)}, u32[]{:S(2)}, u32[]{:S(2)}) collective-permute-start(bf16[2,256,256]{2,1,0:T(8,128)(2,1)S(1)} %bitcast.12), channel_id=1, source_target_pairs={{0,128},{128,0},{1,129},{129,1},{2,130},{130,2},{3,131},{131,3},{4... | collective-permute-start | bytes 786440 | tf_op jit(solution)/shard_map/ppermute | solution.py:200
  13.2 0.0 copy-start
  13.2 0.9 %copy-done = bf16[256,256]{1,0:T(8,128)(2,1)S(1)} copy-done((bf16[256,256]{1,0:T(8,128)(2,1)S(1)}, bf16[256,256]{1,0:T(8,128)(2,1)}, u32[]{:S(2)}) %copy-start) | copy-done | bytes 131096
  14.1 5.8 %first_pass.1 = f32[2,256]{1,0:T(2,128)S(1)} custom-call(bf16[8192,256]{1,0:T(8,128)(2,1)} %centroids.1, bf16[256,256]{1,0:T(8,128)(2,1)S(1)} %copy-done), custom_call_target="tpu_custom_call" | custom-call | flops 1073741824 | bytes 4194304 | tf_op jit(solution)/shard_map/first_pass/pallas_call | solution.py:62
  19.9 0.0 collective-permute-done.across
  19.9 0.7 broadcast_in_dim.3
  20.6 3.3 %collective-permute-start.2 = (bf16[2,256,256]{2,1,0:T(8,128)(2,1)S(1)}, bf16[2,256,256]{2,1,0:T(8,128)(2,1)S(1)}, u32[]{:S(2)}, u32[]{:S(2)}) collective-permute-start(bf16[2,256,256]{2,1,0:T(8,128)(2,1)S(1)} %collective-permute-done.across), channel_id=1, source_target_pairs={{0,128},{128,0},{1,129},{129,1},{2,130},{130,2},{3,131},{131,3},{4... | collective-permute-start | bytes 786440 | tf_op jit(solution)/shard_map/ppermute | solution.py:204
  24.0 8.0 %all-to-all-start = ((f32[64,2,256]{2,1,0:T(2,128)}), f32[64,2,256]{2,1,0:T(2,128)S(1)}, u32[]{:S(2)}, u32[]{:S(2)}) async-start(f32[64,2,256]{2,1,0:T(2,128)} %broadcast_in_dim.3), calls=%async_computation | async-start | bytes 262144 | tf_op jit(solution)/shard_map/all_to_all | solution.py:205
  32.0 1.1 %constant_dynamic-slice_fusion = bf16[2,1,4,1,1,128,256]{6,5,4,3,2,1,0:T(8,128)(2,1)S(1)} fusion(bf16[2,2,4,2,2,128,256]{6,5,4,3,2,1,0:T(8,128)(2,1)} %bitcast.15, s32[]{:T(128)S(6)} %select_n.9, s32[]{:T(128)S(6)} %select_n.10, s32[]{:T(128)S(6)} %select_n.11), kind=kLoop, calls=%fused_computation | loop fusion | bytes 1048588 | tf_op jit(solution)/shard_map/dynamic_slice | solution.py:210
  33.1 0.0 collective-permute-done.1.up
  33.1 9.7 %all-to-all-done = f32[64,2,256]{2,1,0:T(2,128)S(1)} async-done(((f32[64,2,256]{2,1,0:T(2,128)}), f32[64,2,256]{2,1,0:T(2,128)S(1)}, u32[]{:S(2)}, u32[]{:S(2)}) %all-to-all-start) | async-done | bytes 131104 | tf_op jit(solution)/shard_map/all_to_all | solution.py:205
  42.8 0.0 collective-permute-done.2.far
  42.8 3.6 %second_pass.1 = (bf16[8,144,256]{2,1,0:T(8,128)(2,1)S(1)}, f32[1,256]{1,0:T(1,128)}) custom-call(f32[8,8,2,256]{3,2,1,0:T(2,128)S(1)} %bitcast.14, bf16[1024,256]{1,0:T(8,128)(2,1)S(1)} %bitcast.9, bf16[2,256,256]{2,1,0:T(8,128)(2,1)S(1)} %bitcast.13, bf16[2,256,256]{2,1,0:T(8,128)(2,1)S(1)} %collective-permute-done.across, ...), custom_call_target="tpu_custom_call" | custom-call | flops 2147483648 | bytes 1048576 | tf_op jit(solution)/shard_map/second_pass/pallas_call | solution.py:139
  46.5 28.5 %all_to_all.10.parts = bf16[8,144,256]{2,1,0:T(8,128)(2,1)S(1)} all-to-all(bf16[8,144,256]{2,1,0:T(8,128)(2,1)S(1)} %get-tuple-element.8), channel_id=1, replica_groups=mesh['ya'=2,'yb'=2,'za'=4,'zb'=2,'co'=2,'cen'=8] {'ya','za'}, dimensions={0} | all-to-all | bytes 1179648 | tf_op jit(solution)/shard_map/all_to_all | solution.py:213
  75.0 1.1 %last_pass.1 = f32[128,256]{1,0:T(8,128)} custom-call(bf16[8,144,256]{2,1,0:T(8,128)(2,1)S(1)} %all_to_all.10.parts, bf16[8,128,256]{2,1,0:T(8,128)(2,1)S(1)} %bitcast.10), custom_call_target="tpu_custom_call" | custom-call | tf_op jit(solution)/shard_map/last_pass/pallas_call | solution.py:180
Async XLA Ops:
  9.4 10.6 %collective-permute-start = (bf16[2,256,256]{2,1,0:T(8,128)(2,1)S(1)}, bf16[2,256,256]{2,1,0:T(8,128)(2,1)S(1)}, u32[]{:S(2)}, u32[]{:S(2)}) collective-permute-start(bf16[2,256,256]{2,1,0:T(8,128)(2,1)S(1)} %bitcast.11), channel_id=1, source_target_pairs={{0,16},{16,0},{1,17},{17,1},{2,18},{18,2},{3,19},{19,3},{4,20},{20... | collective-permute-start | bytes 786440 | tf_op jit(solution)/shard_map/ppermute | solution.py:199
  11.3 21.8 %collective-permute-start.1 = (bf16[2,256,256]{2,1,0:T(8,128)(2,1)S(1)}, bf16[2,256,256]{2,1,0:T(8,128)(2,1)S(1)}, u32[]{:S(2)}, u32[]{:S(2)}) collective-permute-start(bf16[2,256,256]{2,1,0:T(8,128)(2,1)S(1)} %bitcast.12), channel_id=1, source_target_pairs={{0,128},{128,0},{1,129},{129,1},{2,130},{130,2},{3,131},{131,3},{4... | collective-permute-start | bytes 786440 | tf_op jit(solution)/shard_map/ppermute | solution.py:200
  13.2 0.9 %copy-start = (bf16[256,256]{1,0:T(8,128)(2,1)S(1)}, bf16[256,256]{1,0:T(8,128)(2,1)}, u32[]{:S(2)}) copy-start(bf16[256,256]{1,0:T(8,128)(2,1)} %rows.1) | copy-start | bytes 393220
  20.6 22.2 %collective-permute-start.2 = (bf16[2,256,256]{2,1,0:T(8,128)(2,1)S(1)}, bf16[2,256,256]{2,1,0:T(8,128)(2,1)S(1)}, u32[]{:S(2)}, u32[]{:S(2)}) collective-permute-start(bf16[2,256,256]{2,1,0:T(8,128)(2,1)S(1)} %collective-permute-done.across), channel_id=1, source_target_pairs={{0,128},{128,0},{1,129},{129,1},{2,130},{130,2},{3,131},{131,3},{4... | collective-permute-start | bytes 786440 | tf_op jit(solution)/shard_map/ppermute | solution.py:204
  24.0 18.8 %all-to-all-start = ((f32[64,2,256]{2,1,0:T(2,128)}), f32[64,2,256]{2,1,0:T(2,128)S(1)}, u32[]{:S(2)}, u32[]{:S(2)}) async-start(f32[64,2,256]{2,1,0:T(2,128)} %broadcast_in_dim.3), calls=%async_computation | async-start | bytes 262144 | tf_op jit(solution)/shard_map/all_to_all | solution.py:205

commit v3 on v2

--- a/solution.py
+++ b/solution.py
@@ -1,3 +1,5 @@
+import functools
+
 import jax
 import jax.numpy as jnp
 from jax import lax
@@ -6,10 +8,11 @@
 from jax.sharding import Mesh
 from jax.sharding import PartitionSpec as P
 
-AXES = ("ya", "yb", "za", "zb", "co")
-GATHER = ("yb", "zb", "co")
-REDUCE = ("ya", "za")
-CEN = "cen"
+AXES = ("yl", "z", "co")
+CEN = ("x", "yh")
+GATHER = ("yl", "co")
+REDUCE = "z"
+RING = ("yl", "yh")
 MIB = 1 << 20
 CHUNK = 1024
 inv_temp = 0.0625
@@ -40,24 +43,22 @@
     for i in range(chunks):
         copy(i).start()
 
-    def step(i, carry):
-        peak, total = carry
+    own = rows[lax.axis_index("co")]
+    found = []
+    for i in range(chunks):
         copy(i).wait()
-        block = table[pl.ds(pl.multiple_of(i * CHUNK, CHUNK), CHUNK), :]
-        logits = products(block, rows[...]) - squares(block)
-        top = jnp.maximum(peak, jnp.max(logits, axis=0, keepdims=True))
-        total = total * jnp.exp(peak - top) + jnp.sum(jnp.exp(logits - top), axis=0, keepdims=True)
-        return top, total
-
-    n = rows.shape[0]
-    start = (jnp.full((1, n), -jnp.inf, jnp.float32), jnp.zeros((1, n), jnp.float32))
-    peak, total = lax.fori_loop(0, chunks, step, start)
+        block = table[i * CHUNK : (i + 1) * CHUNK, :]
+        logits = products(block, own) - squares(block)
+        top = jnp.max(logits, axis=0, keepdims=True)
+        found.append((top, jnp.sum(jnp.exp(logits - top), axis=0, keepdims=True)))
+    peak = functools.reduce(jnp.maximum, [top for top, _ in found])
+    total = sum(part * jnp.exp(top - peak) for top, part in found)
     stats[0:1, :] = peak
     stats[1:2, :] = total
 
 
-def first_pass(points, centroids):
-    n, d = points.shape
+def first_pass(near, centroids):
+    _, n, d = near.shape
     k = centroids.shape[0]
     return pl.pallas_call(
         first_kernel,
@@ -76,11 +77,11 @@
             flops=2 * n * k * d, bytes_accessed=2 * k * d, transcendentals=n * k
         ),
         name="first_pass",
-    )(pltpu.with_memory_space_constraint(centroids, pltpu.HBM), points)
-
-
-def second_kernel(stats, table, near, across, up, far, parts, own_norm, log_norms, sums, masses):
-    yb, zb, co = (lax.axis_index(a) for a in GATHER)
+    )(pltpu.with_memory_space_constraint(centroids, pltpu.HBM), near)
+
+
+def second_kernel(stats, table, near, above, below, far, parts, own_norm, log_norms, sums, masses):
+    yl, co = (lax.axis_index(a) for a in GATHER)
 
     cen = stats.shape[0]
     peak = stats[0, :, 0, :]
@@ -90,13 +91,13 @@
     for c in range(1, cen):
         total = total + stats[c, :, 1, :] * jnp.exp(stats[c, :, 0, :] - peak)
     log_norms[...] = peak + jnp.log(total)
-    own_norm[...] = log_norms[pl.ds((yb * 2 + zb) * 2 + co, 1), :]
+    own_norm[...] = log_norms[pl.ds(yl * 2 + co, 1), :]
 
     norms = squares(table[...])
-    pairs = ((near, yb, zb), (across, yb, 1 - zb), (up, 1 - yb, zb), (far, 1 - yb, 1 - zb))
-    for at, (rows, y, z) in enumerate(pairs):
+    pairs = ((near, 0), (below, 3), (above, 1), (far, 2))
+    for at, (rows, off) in enumerate(pairs):
         for c in range(2):
-            shift = log_norms[pl.ds((y * 2 + z) * 2 + c, 1), :]
+            shift = log_norms[pl.ds(lax.rem(yl + off, 4) * 2 + c, 1), :]
             logits = products(table[...], rows[c]) - norms
             shares = jnp.exp(logits - shift).astype(jnp.bfloat16)
             product = lax.dot_general(
@@ -159,7 +160,7 @@
 
 def last_kernel(parts, table, updated):
     owned = updated.shape[0]
-    own = table[lax.axis_index("ya") * lax.axis_size("za") + lax.axis_index("za")]
+    own = table[lax.axis_index(REDUCE)]
     sums = own.astype(jnp.float32)
     masses = jnp.ones((owned, owned), jnp.float32)
     for r in range(parts.shape[0]):
@@ -187,36 +188,39 @@
     )(parts, table)
 
 
+def moved(array, hops):
+    low, high = (lax.axis_size(a) for a in RING)
+    place = [(y % low) * high + y // low for y in range(low * high)]
+    pairs = [(place[y], place[(y + hops) % (low * high)]) for y in range(low * high)]
+    return lax.ppermute(array, RING, pairs)
+
+
 def body(points, centroids):
     n, d = points.shape
     cen = lax.axis_size(CEN)
     gathered = lax.axis_size(GATHER)
     reduced = lax.axis_size(REDUCE)
     owned = centroids.shape[0] // (gathered * reduced)
-    swap = [(0, 1), (1, 0)]
 
     near = lax.all_gather(points, "co")
-    across = lax.ppermute(near, "zb", swap)
-    up = lax.ppermute(near, "yb", swap)
-    stats = first_pass(points, centroids)
+    below, above, far = moved(near, 1), moved(near, -1), moved(near, 2)
+    stats = first_pass(near, centroids)
     copies = jnp.broadcast_to(stats, (cen * gathered, 2, n))
-    across, copies = lax.optimization_barrier((across, copies))
-    far = lax.ppermute(across, "yb", swap)
-    every = lax.all_to_all(copies, (CEN, *GATHER), 0, 0, tiled=True)
+    every = lax.all_to_all(copies, (*CEN, *GATHER), 0, 0, tiled=True)
     every = every.reshape(cen, gathered, 2, n)
     sizes = [lax.axis_size(a) for a in AXES]
-    at = (0, lax.axis_index("yb"), 0, lax.axis_index("zb"), lax.axis_index("co"), 0, 0)
-    cut = (sizes[0], 1, sizes[2], 1, 1, owned, d)
-    table = lax.dynamic_slice(centroids.reshape(*sizes, owned, d), at, cut)
-    table = table.reshape(reduced, owned, d)
-    parts, log_norm = second_pass(every, table, (near, across, up, far))
+    at = (lax.axis_index("yl"), 0, lax.axis_index("co"), 0, 0)
+    table = lax.dynamic_slice(
+        centroids.reshape(*sizes, owned, d), at, (1, reduced, 1, owned, d)
+    )
+    table = lax.optimization_barrier(table.reshape(reduced, owned, d))
+    parts, log_norm = second_pass(every, table, (near, above, below, far))
     parts = lax.all_to_all(parts, REDUCE, 0, 0, tiled=True)
     return last_pass(parts, table), log_norm[0]
 
 
 def solution(mesh):
-    shape = (2, 2, 4, 2, 2, mesh.shape["cen"])
-    torus = Mesh(mesh.devices.reshape(shape), (*AXES, CEN))
+    torus = Mesh(mesh.devices.reshape(4, 8, 2, 4, 2), (*AXES, *CEN))
     in_specs = (P(AXES, None), P(CEN, None))
-    out_specs = (P((CEN, *AXES), None), P(AXES))
+    out_specs = (P((*CEN, *AXES), None), P(AXES))
     return jax.shard_map(body, mesh=torus, in_specs=in_specs, out_specs=out_specs, check_vma=False)

time: 76.5 us -> 75.2 us (0.983)
  local copies, waits for them, and re-layouts: 2.68 us -> 1.78 us
  Pallas kernels: 10.5 us -> 11.3 us
    all_to_all x1, starting transfers between devices: 8.03 us -> 6.44 us  [body(): every = lax.all_to_all(copies, (*CEN, *GATHER), 0, 0, tiled=True)]
    ppermute x3, starting transfers between devices: 7.18 us -> 8.4 us  [moved(): return lax.ppermute(array, RING, pairs)]
    dynamic_slice x1 -> x0, local copies, waits for them, and re-layouts: 1.09 us -> none  [body(): table = lax.dynamic_slice(centroids.reshape(*sizes, owned, d), at, cut)]
    reshape x0 -> x1, local copies, waits for them, and re-layouts: none -> 1.09 us  [body(): table = lax.optimization_barrier(table.reshape(reduced, owned, d))]
    unnamed x2 -> x0, local copies, waits for them, and re-layouts: 0.9 us -> none
    pallas_call x1, Pallas kernels: 5.8 us -> 6.6 us  [first_pass(): pl.pallas_call(first_kernel, in_specs=[pl.BlockSpec(memory_space=pltpu.HB...]
  transfers between devices with their start and end apart: 4 -> 4, of which waited for: 1 -> 1; matrix products, arithmetic and copies ran while one was open for 2% -> 2% of each run, Pallas kernels for 8% -> 9%
where the time goes in v3:
time: 75.2 us; the launch traced here: 74.8 us
  blocking collectives  36.9 us (49%)
  starting transfers between devices  14.8 us (20%)
  Pallas kernels  11.3 us (15%)
  waiting for transfers between devices  9.28 us (12%)
  local copies, waits for them, and re-layouts  1.78 us (2%)
    all_to_all x1, blocking collectives, body(): parts = lax.all_to_all(parts, REDUCE, 0, 0, tiled=True)  28.2 us
    all_to_all x1, waiting for transfers between devices, body(): every = lax.all_to_all(copies, (*CEN, *GATHER), 0, 0, tiled=True)  9.27 us
    all_gather x1, blocking collectives, body(): near = lax.all_gather(points, 'co')  8.72 us
    ppermute x3, starting transfers between devices, moved(): return lax.ppermute(array, RING, pairs)  8.4 us
    pallas_call x1, Pallas kernels, first_pass(): pl.pallas_call(first_kernel, in_specs=[pl.BlockSpec(memory_space=pltpu.HB...  6.6 us
    all_to_all x1, starting transfers between devices, body(): every = lax.all_to_all(copies, (*CEN, *GATHER), 0, 0, tiled=True)  6.44 us
    pallas_call x1, Pallas kernels, second_pass(): pl.pallas_call(second_kernel, in_specs=[pl.BlockSpec(memory_space=pltpu.V...  3.65 us
  transfers between devices with their start and end apart: 4, of which 1 were waited for; matrix products, arithmetic and copies ran while one was open for 2% of the time, Pallas kernels for 9%

profile of v3, /device:TPU:1, one launch (start us, length us, event | category | flops | bytes accessed | tf_op | source)
XLA Modules:
  0.0 74.8 jit_solution(8323963060417513828)
XLA Ops:
  0.6 8.7 %all-gather = bf16[512,256]{1,0:T(8,128)(2,1)S(1)} all-gather(bf16[256,256]{1,0:T(8,128)(2,1)} %param.2), channel_id=2, replica_groups=mesh['yl'=4,'z'=8,'co'=2,'x'=4,'yh'=2] {'co'}, dimensions={0}, use_global_device_ids=true | all-gather | bytes 393216 | tf_op jit(solution)/shard_map/all_gather | solution.py:205
  9.4 1.9 %collective-permute-start.2 = (bf16[2,256,256]{2,1,0:T(8,128)(2,1)S(1)}, bf16[2,256,256]{2,1,0:T(8,128)(2,1)S(1)}, u32[]{:S(2)}, u32[]{:S(2)}) collective-permute-start(bf16[2,256,256]{2,1,0:T(8,128)(2,1)S(1)} %bitcast.10), channel_id=1, source_target_pairs={{0,256},{128,384},{256,1},{384,129},{1,257},{129,385},{257,0},{385... | collective-permute-start | bytes 786440 | tf_op jit(solution)/shard_map/ppermute | solution.py:195
  11.3 1.9 %collective-permute-start.1 = (bf16[2,256,256]{2,1,0:T(8,128)(2,1)S(1)}, bf16[2,256,256]{2,1,0:T(8,128)(2,1)S(1)}, u32[]{:S(2)}, u32[]{:S(2)}) collective-permute-start(bf16[2,256,256]{2,1,0:T(8,128)(2,1)S(1)} %bitcast.11), channel_id=1, source_target_pairs={{0,128},{128,256},{256,384},{384,1},{1,129},{129,257},{257,385},{3... | collective-permute-start | bytes 786440 | tf_op jit(solution)/shard_map/ppermute | solution.py:195
  13.2 4.6 %collective-permute-start = (bf16[2,256,256]{2,1,0:T(8,128)(2,1)S(1)}, bf16[2,256,256]{2,1,0:T(8,128)(2,1)S(1)}, u32[]{:S(2)}, u32[]{:S(2)}) collective-permute-start(bf16[2,256,256]{2,1,0:T(8,128)(2,1)S(1)} %bitcast.12), channel_id=1, source_target_pairs={{0,385},{128,0},{256,128},{384,256},{1,384},{129,1},{257,129},{385... | collective-permute-start | bytes 786440 | tf_op jit(solution)/shard_map/ppermute | solution.py:195
  17.8 6.6 %first_pass.1 = f32[2,256]{1,0:T(2,128)S(1)} custom-call(bf16[8192,256]{1,0:T(8,128)(2,1)} %centroids.1, bf16[2,256,256]{2,1,0:T(8,128)(2,1)S(1)} %bitcast.13), custom_call_target="tpu_custom_call" | custom-call | flops 1073741824 | bytes 4194304 | tf_op jit(solution)/shard_map/first_pass/pallas_call | solution.py:63
  24.4 0.7 broadcast_in_dim.3
  25.1 6.4 %all-to-all-start = ((f32[64,2,256]{2,1,0:T(2,128)}), f32[64,2,256]{2,1,0:T(2,128)S(1)}, u32[]{:S(2)}, u32[]{:S(2)}) async-start(f32[64,2,256]{2,1,0:T(2,128)} %broadcast_in_dim.3), calls=%async_computation | async-start | bytes 262144 | tf_op jit(solution)/shard_map/all_to_all | solution.py:209
  31.5 1.1 %dynamic-slice_bitcast_fusion.table = bf16[8,128,256]{2,1,0:T(8,128)(2,1)S(1)} fusion(bf16[4,8,2,128,256]{4,3,2,1,0:T(8,128)(2,1)} %bitcast.16, s32[]{:T(128)S(6)} %select_n.6, s32[]{:T(128)S(6)} %select_n.7), kind=kLoop, calls=%fused_computation | loop fusion | bytes 1048584 | tf_op jit(solution)/shard_map/reshape | solution.py:216
  32.6 9.3 %all-to-all-done = f32[64,2,256]{2,1,0:T(2,128)S(1)} async-done(((f32[64,2,256]{2,1,0:T(2,128)}), f32[64,2,256]{2,1,0:T(2,128)S(1)}, u32[]{:S(2)}, u32[]{:S(2)}) %all-to-all-start) | async-done | bytes 131104 | tf_op jit(solution)/shard_map/all_to_all | solution.py:209
  41.9 0.0 collective-permute-done.2.far
  41.9 0.0 collective-permute-done.1.below
  41.9 0.0 collective-permute-done.above
  41.9 3.6 %second_pass.1 = (bf16[8,144,256]{2,1,0:T(8,128)(2,1)S(1)}, f32[1,256]{1,0:T(1,128)}) custom-call(f32[8,8,2,256]{3,2,1,0:T(2,128)S(1)} %bitcast.15, bf16[1024,256]{1,0:T(8,128)(2,1)S(1)} %bitcast.9, bf16[2,256,256]{2,1,0:T(8,128)(2,1)S(1)} %bitcast.14, bf16[2,256,256]{2,1,0:T(8,128)(2,1)S(1)} %collective-permute-done.above, ...), custom_call_target="tpu_custom_call" | custom-call | flops 2147483648 | bytes 1048576 | tf_op jit(solution)/shard_map/second_pass/pallas_call | solution.py:140
  45.6 28.2 %all_to_all.10.parts = bf16[8,144,256]{2,1,0:T(8,128)(2,1)S(1)} all-to-all(bf16[8,144,256]{2,1,0:T(8,128)(2,1)S(1)} %get-tuple-element.4), channel_id=1, replica_groups=mesh['yl'=4,'z'=8,'co'=2,'x'=4,'yh'=2] {'z'}, dimensions={0} | all-to-all | bytes 1179648 | tf_op jit(solution)/shard_map/all_to_all | solution.py:218
  73.7 1.1 %last_pass.1 = f32[128,256]{1,0:T(8,128)} custom-call(bf16[8,144,256]{2,1,0:T(8,128)(2,1)S(1)} %all_to_all.10.parts, bf16[8,128,256]{2,1,0:T(8,128)(2,1)S(1)} %dynamic-slice_bitcast_fusion.table), custom_call_target="tpu_custom_call" | custom-call | tf_op jit(solution)/shard_map/last_pass/pallas_call | solution.py:181
Async XLA Ops:
  9.4 32.5 %collective-permute-start.2 = (bf16[2,256,256]{2,1,0:T(8,128)(2,1)S(1)}, bf16[2,256,256]{2,1,0:T(8,128)(2,1)S(1)}, u32[]{:S(2)}, u32[]{:S(2)}) collective-permute-start(bf16[2,256,256]{2,1,0:T(8,128)(2,1)S(1)} %bitcast.10), channel_id=1, source_target_pairs={{0,256},{128,384},{256,1},{384,129},{1,257},{129,385},{257,0},{385... | collective-permute-start | bytes 786440 | tf_op jit(solution)/shard_map/ppermute | solution.py:195
  11.3 30.6 %collective-permute-start.1 = (bf16[2,256,256]{2,1,0:T(8,128)(2,1)S(1)}, bf16[2,256,256]{2,1,0:T(8,128)(2,1)S(1)}, u32[]{:S(2)}, u32[]{:S(2)}) collective-permute-start(bf16[2,256,256]{2,1,0:T(8,128)(2,1)S(1)} %bitcast.11), channel_id=1, source_target_pairs={{0,128},{128,256},{256,384},{384,1},{1,129},{129,257},{257,385},{3... | collective-permute-start | bytes 786440 | tf_op jit(solution)/shard_map/ppermute | solution.py:195
  13.2 28.7 %collective-permute-start = (bf16[2,256,256]{2,1,0:T(8,128)(2,1)S(1)}, bf16[2,256,256]{2,1,0:T(8,128)(2,1)S(1)}, u32[]{:S(2)}, u32[]{:S(2)}) collective-permute-start(bf16[2,256,256]{2,1,0:T(8,128)(2,1)S(1)} %bitcast.12), channel_id=1, source_target_pairs={{0,385},{128,0},{256,128},{384,256},{1,384},{129,1},{257,129},{385... | collective-permute-start | bytes 786440 | tf_op jit(solution)/shard_map/ppermute | solution.py:195
  25.1 16.8 %all-to-all-start = ((f32[64,2,256]{2,1,0:T(2,128)}), f32[64,2,256]{2,1,0:T(2,128)S(1)}, u32[]{:S(2)}, u32[]{:S(2)}) async-start(f32[64,2,256]{2,1,0:T(2,128)} %broadcast_in_dim.3), calls=%async_computation | async-start | bytes 262144 | tf_op jit(solution)/shard_map/all_to_all | solution.py:209

commit v4 on v3

--- a/solution.py
+++ b/solution.py
@@ -1,5 +1,3 @@
-import functools
-
 import jax
 import jax.numpy as jnp
 from jax import lax
@@ -12,9 +10,9 @@
 CEN = ("x", "yh")
 GATHER = ("yl", "co")
 REDUCE = "z"
-RING = ("yl", "yh")
+RING = ("yl", "co", "yh")
 MIB = 1 << 20
-CHUNK = 1024
+CHUNK = 2048
 inv_temp = 0.0625
 SPAN, FLOOR = 240.0, 120.0
 
@@ -33,54 +31,59 @@
     )
 
 
-def first_kernel(centroids, rows, stats, table, arrived):
+def first_kernel(centroids, points, stats, table, rows, arrived, ready):
     chunks = table.shape[0] // CHUNK
 
     def copy(i):
         here = pl.ds(i * CHUNK, CHUNK)
         return pltpu.make_async_copy(centroids.at[here], table.at[here], arrived.at[i])
 
+    own = pltpu.make_async_copy(points, rows, ready)
+    own.start()
     for i in range(chunks):
         copy(i).start()
-
-    own = rows[lax.axis_index("co")]
-    found = []
-    for i in range(chunks):
+    own.wait()
+
+    def step(i, carry):
+        peak, total = carry
         copy(i).wait()
-        block = table[i * CHUNK : (i + 1) * CHUNK, :]
-        logits = products(block, own) - squares(block)
-        top = jnp.max(logits, axis=0, keepdims=True)
-        found.append((top, jnp.sum(jnp.exp(logits - top), axis=0, keepdims=True)))
-    peak = functools.reduce(jnp.maximum, [top for top, _ in found])
-    total = sum(part * jnp.exp(top - peak) for top, part in found)
-    stats[0:1, :] = peak
-    stats[1:2, :] = total
-
-
-def first_pass(near, centroids):
-    _, n, d = near.shape
+        block = table[pl.ds(pl.multiple_of(i * CHUNK, CHUNK), CHUNK), :]
+        logits = products(block, rows[...]) - squares(block)
+        top = jnp.maximum(peak, jnp.max(logits, axis=0, keepdims=True))
+        total = total * jnp.exp(peak - top) + jnp.sum(jnp.exp(logits - top), axis=0, keepdims=True)
+        return top, total
+
+    n = rows.shape[0]
+    start = (jnp.full((1, n), -jnp.inf, jnp.float32), jnp.zeros((1, n), jnp.float32))
+    peak, total = lax.fori_loop(0, chunks, step, start)
+    both = jnp.concatenate([peak, total], axis=0)
+    for i in range(stats.shape[0]):
+        stats[i] = both
+
+
+def first_pass(points, centroids, receivers):
+    n, d = points.shape
     k = centroids.shape[0]
     return pl.pallas_call(
         first_kernel,
-        in_specs=[
-            pl.BlockSpec(memory_space=pltpu.HBM),
-            pl.BlockSpec(memory_space=pltpu.VMEM),
-        ],
+        in_specs=[pl.BlockSpec(memory_space=pltpu.HBM)] * 2,
         out_specs=pl.BlockSpec(memory_space=pltpu.VMEM),
-        out_shape=jax.ShapeDtypeStruct((2, n), jnp.float32),
+        out_shape=jax.ShapeDtypeStruct((receivers, 2, n), jnp.float32),
         scratch_shapes=[
             pltpu.VMEM((k, d), centroids.dtype),
+            pltpu.VMEM((n, d), points.dtype),
             pltpu.SemaphoreType.DMA((k // CHUNK,)),
+            pltpu.SemaphoreType.DMA,
         ],
-        compiler_params=pltpu.CompilerParams(vmem_limit_bytes=20 * MIB),
+        compiler_params=pltpu.CompilerParams(vmem_limit_bytes=24 * MIB),
         cost_estimate=pl.CostEstimate(
             flops=2 * n * k * d, bytes_accessed=2 * k * d, transcendentals=n * k
         ),
         name="first_pass",
-    )(pltpu.with_memory_space_constraint(centroids, pltpu.HBM), near)
-
-
-def second_kernel(stats, table, near, above, below, far, parts, own_norm, log_norms, sums, masses):
+    )(*(pltpu.with_memory_space_constraint(a, pltpu.HBM) for a in (centroids, points)))
+
+
+def second_kernel(stats, table, near, sides, far, parts, own_norm, log_norms, sums, masses):
     yl, co = (lax.axis_index(a) for a in GATHER)
 
     cen = stats.shape[0]
@@ -94,7 +97,7 @@
     own_norm[...] = log_norms[pl.ds(yl * 2 + co, 1), :]
 
     norms = squares(table[...])
-    pairs = ((near, 0), (below, 3), (above, 1), (far, 2))
+    pairs = ((near, 0), (sides.at[0], 3), (sides.at[1], 1), (far, 2))
     for at, (rows, off) in enumerate(pairs):
         for c in range(2):
             shift = log_norms[pl.ds(lax.rem(yl + off, 4) * 2 + c, 1), :]
@@ -139,7 +142,7 @@
     k = owned * reduced
     return pl.pallas_call(
         second_kernel,
-        in_specs=[pl.BlockSpec(memory_space=pltpu.VMEM)] * 6,
+        in_specs=[pl.BlockSpec(memory_space=pltpu.VMEM)] * 5,
         out_specs=[pl.BlockSpec(memory_space=pltpu.VMEM)] * 2,
         out_shape=[
             jax.ShapeDtypeStruct((reduced, owned + 16, d), jnp.bfloat16),
@@ -189,9 +192,17 @@
 
 
 def moved(array, hops):
-    low, high = (lax.axis_size(a) for a in RING)
-    place = [(y % low) * high + y // low for y in range(low * high)]
-    pairs = [(place[y], place[(y + hops) % (low * high)]) for y in range(low * high)]
+    low, cores, high = (lax.axis_size(a) for a in RING)
+    ring = low * high
+
+    def place(y, core):
+        return ((y % low) * cores + core) * high + y // low
+
+    pairs = [
+        (place(y, core), place((y + hops[core]) % ring, core))
+        for y in range(ring)
+        for core in range(cores)
+    ]
     return lax.ppermute(array, RING, pairs)
 
 
@@ -202,11 +213,14 @@
     reduced = lax.axis_size(REDUCE)
     owned = centroids.shape[0] // (gathered * reduced)
 
+    far = moved(points, (2, -2))
     near = lax.all_gather(points, "co")
-    below, above, far = moved(near, 1), moved(near, -1), moved(near, 2)
-    stats = first_pass(near, centroids)
-    copies = jnp.broadcast_to(stats, (cen * gathered, 2, n))
-    every = lax.all_to_all(copies, (*CEN, *GATHER), 0, 0, tiled=True)
+    side = moved(near, (1, -1))
+    stats = first_pass(points, centroids, cen * gathered)
+    far, side, _ = lax.optimization_barrier((far, side, stats))
+    sides = lax.all_gather(side, "co")
+    far = lax.all_gather(far, "co")
+    every = lax.all_to_all(stats, (*CEN, *GATHER), 0, 0, tiled=True)
     every = every.reshape(cen, gathered, 2, n)
     sizes = [lax.axis_size(a) for a in AXES]
     at = (lax.axis_index("yl"), 0, lax.axis_index("co"), 0, 0)
@@ -214,7 +228,7 @@
         centroids.reshape(*sizes, owned, d), at, (1, reduced, 1, owned, d)
     )
     table = lax.optimization_barrier(table.reshape(reduced, owned, d))
-    parts, log_norm = second_pass(every, table, (near, above, below, far))
+    parts, log_norm = second_pass(every, table, (near, sides, far))
     parts = lax.all_to_all(parts, REDUCE, 0, 0, tiled=True)
     return last_pass(parts, table), log_norm[0]
 

time: 75.2 us -> 69.9 us (0.930)
  waiting for transfers between devices: 9.28 us -> 4.99 us
  starting transfers between devices: 14.8 us -> 11.6 us
  blocking collectives: 36.9 us -> 39.9 us
    ppermute x3 -> x2, starting transfers between devices: 8.4 us -> 3.83 us  [moved(): return lax.ppermute(array, RING, pairs)]
    all_to_all x1, waiting for transfers between devices: 9.27 us -> 4.99 us  [body(): every = lax.all_to_all(stats, (*CEN, *GATHER), 0, 0, tiled=True)]
    all_gather x0 -> x2, blocking collectives: none -> 4.26 us  [the longest x1 2.17 us: body(): sides = lax.all_gather(side, 'co')]
    all_to_all x1, starting transfers between devices: 6.44 us -> 7.78 us  [body(): every = lax.all_to_all(stats, (*CEN, *GATHER), 0, 0, tiled=True)]
    all_to_all x1, blocking collectives: 28.2 us -> 27 us  [body(): parts = lax.all_to_all(parts, REDUCE, 0, 0, tiled=True)]
  transfers between devices with their start and end apart: 4 -> 3, of which waited for: 1 -> 1; matrix products, arithmetic and copies ran while one was open for 2% -> 2% of each run, Pallas kernels for 9% -> 9%
where the time goes in v4:
time: 69.9 us; the launch traced here: 69.5 us
  blocking collectives  39.9 us (57%)
  starting transfers between devices  11.6 us (17%)
  Pallas kernels  11.2 us (16%)
  waiting for transfers between devices  4.99 us (7%)
  local copies, waits for them, and re-layouts  1.09 us (2%)
    all_to_all x1, blocking collectives, body(): parts = lax.all_to_all(parts, REDUCE, 0, 0, tiled=True)  27 us
    all_gather x1, blocking collectives, body(): near = lax.all_gather(points, 'co')  8.72 us
    all_to_all x1, starting transfers between devices, body(): every = lax.all_to_all(stats, (*CEN, *GATHER), 0, 0, tiled=True)  7.78 us
    pallas_call x1, Pallas kernels, first_pass(): pl.pallas_call(first_kernel, in_specs=[pl.BlockSpec(memory_space=pltpu.HB...  6.47 us
    all_to_all x1, waiting for transfers between devices, body(): every = lax.all_to_all(stats, (*CEN, *GATHER), 0, 0, tiled=True)  4.99 us
    ppermute x2, starting transfers between devices, moved(): return lax.ppermute(array, RING, pairs)  3.83 us
    pallas_call x1, Pallas kernels, second_pass(): pl.pallas_call(second_kernel, in_specs=[pl.BlockSpec(memory_space=pltpu.V...  3.64 us
    all_gather x1, blocking collectives, body(): sides = lax.all_gather(side, 'co')  2.17 us
  transfers between devices with their start and end apart: 3, of which 1 were waited for; matrix products, arithmetic and copies ran while one was open for 2% of the time, Pallas kernels for 9%

profile of v4, /device:TPU:1, one launch (start us, length us, event | category | flops | bytes accessed | tf_op | source)
XLA Modules:
  0.0 69.5 jit_solution(10383744593163499719)
XLA Ops:
  0.6 8.7 %all-gather = bf16[512,256]{1,0:T(8,128)(2,1)S(1)} all-gather(bf16[256,256]{1,0:T(8,128)(2,1)} %points.1), channel_id=2, replica_groups=mesh['yl'=4,'z'=8,'co'=2,'x'=4,'yh'=2] {'co'}, dimensions={0}, use_global_device_ids=true | all-gather | bytes 393216 | tf_op jit(solution)/shard_map/all_gather | solution.py:217
  9.4 1.9 %collective-permute-start.1 = (bf16[2,256,256]{2,1,0:T(8,128)(2,1)S(1)}, bf16[2,256,256]{2,1,0:T(8,128)(2,1)S(1)}, u32[]{:S(2)}, u32[]{:S(2)}) collective-permute-start(bf16[2,256,256]{2,1,0:T(8,128)(2,1)S(1)} %bitcast.13), channel_id=1, source_target_pairs={{0,128},{8,393},{128,256},{136,8},{256,384},{264,136},{384,1},{392... | collective-permute-start | bytes 786440 | tf_op jit(solution)/shard_map/ppermute | solution.py:206
  11.3 1.9 %collective-permute-start = (bf16[256,256]{1,0:T(8,128)(2,1)}, bf16[256,256]{1,0:T(8,128)(2,1)S(1)}, u32[]{:S(2)}, u32[]{:S(2)}) collective-permute-start(bf16[256,256]{1,0:T(8,128)(2,1)} %points.1), channel_id=1, source_target_pairs={{0,256},{8,265},{128,384},{136,393},{256,1},{264,8},{384,129},{392... | collective-permute-start | bytes 393224 | tf_op jit(solution)/shard_map/ppermute | solution.py:206
  13.2 6.5 %first_pass.1 = f32[64,2,256]{2,1,0:T(2,128)} custom-call(bf16[8192,256]{1,0:T(8,128)(2,1)} %centroids.1, bf16[256,256]{1,0:T(8,128)(2,1)} %points.1), custom_call_target="tpu_custom_call" | custom-call | flops 1073741824 | bytes 4194304 | tf_op jit(solution)/shard_map/first_pass/pallas_call | solution.py:67
  19.7 7.8 %all-to-all-start = ((f32[64,2,256]{2,1,0:T(2,128)}), f32[64,2,256]{2,1,0:T(2,128)S(1)}, u32[]{:S(2)}, u32[]{:S(2)}) async-start(f32[64,2,256]{2,1,0:T(2,128)} %first_pass.1), calls=%async_computation | async-start | bytes 262144 | tf_op jit(solution)/shard_map/all_to_all | solution.py:223
  27.5 1.1 %dynamic-slice_bitcast_fusion.table = bf16[8,128,256]{2,1,0:T(8,128)(2,1)S(1)} fusion(bf16[4,8,2,128,256]{4,3,2,1,0:T(8,128)(2,1)} %bitcast.17, s32[]{:T(128)S(6)} %select_n.6, s32[]{:T(128)S(6)} %select_n.7), kind=kLoop, calls=%fused_computation | loop fusion | bytes 1048584 | tf_op jit(solution)/shard_map/reshape | solution.py:230
  28.6 0.0 collective-permute-done
  28.6 0.0 collective-permute-done.1
  28.6 2.1 %all-gather.2 = bf16[512,256]{1,0:T(8,128)(2,1)S(1)} all-gather(bf16[256,256]{1,0:T(8,128)(2,1)S(1)} %collective-permute-done), channel_id=4, replica_groups=mesh['yl'=4,'z'=8,'co'=2,'x'=4,'yh'=2] {'co'}, dimensions={0}, use_global_device_ids=true | all-gather | bytes 393216 | tf_op jit(solution)/shard_map/all_gather | solution.py:222
  30.7 2.2 %all-gather.1 = bf16[4,256,256]{2,1,0:T(8,128)(2,1)S(1)} all-gather(bf16[2,256,256]{2,1,0:T(8,128)(2,1)S(1)} %collective-permute-done.1), channel_id=3, replica_groups=mesh['yl'=4,'z'=8,'co'=2,'x'=4,'yh'=2] {'co'}, dimensions={0}, use_global_device_ids=true | all-gather | bytes 786432 | tf_op jit(solution)/shard_map/all_gather | solution.py:221
  32.8 5.0 %all-to-all-done = f32[64,2,256]{2,1,0:T(2,128)S(1)} async-done(((f32[64,2,256]{2,1,0:T(2,128)}), f32[64,2,256]{2,1,0:T(2,128)S(1)}, u32[]{:S(2)}, u32[]{:S(2)}) %all-to-all-start) | async-done | bytes 131104 | tf_op jit(solution)/shard_map/all_to_all | solution.py:223
  37.8 3.6 %second_pass.1 = (bf16[8,144,256]{2,1,0:T(8,128)(2,1)S(1)}, f32[1,256]{1,0:T(1,128)}) custom-call(f32[8,8,2,256]{3,2,1,0:T(2,128)S(1)} %bitcast.16, bf16[1024,256]{1,0:T(8,128)(2,1)S(1)} %bitcast.11, bf16[2,256,256]{2,1,0:T(8,128)(2,1)S(1)} %bitcast.14, bf16[2,2,256,256]{3,2,1,0:T(8,128)(2,1)S(1)} %bitcast.12, bf16[2,256,256]{2,1,0:T(8,128)(2,1)S(1)} %bitcast.15), custom_call_target="tpu_custom_call" | custom-call | flops 2147483648 | bytes 1048576 | tf_op jit(solution)/shard_map/second_pass/pallas_call | solution.py:143
  41.5 27.0 %all_to_all.10.parts = bf16[8,144,256]{2,1,0:T(8,128)(2,1)S(1)} all-to-all(bf16[8,144,256]{2,1,0:T(8,128)(2,1)S(1)} %get-tuple-element.8), channel_id=1, replica_groups=mesh['yl'=4,'z'=8,'co'=2,'x'=4,'yh'=2] {'z'}, dimensions={0} | all-to-all | bytes 1179648 | tf_op jit(solution)/shard_map/all_to_all | solution.py:232
  68.4 1.1 %last_pass.1 = f32[128,256]{1,0:T(8,128)} custom-call(bf16[8,144,256]{2,1,0:T(8,128)(2,1)S(1)} %all_to_all.10.parts, bf16[8,128,256]{2,1,0:T(8,128)(2,1)S(1)} %dynamic-slice_bitcast_fusion.table), custom_call_target="tpu_custom_call" | custom-call | tf_op jit(solution)/shard_map/last_pass/pallas_call | solution.py:184
Async XLA Ops:
  9.4 19.2 %collective-permute-start.1 = (bf16[2,256,256]{2,1,0:T(8,128)(2,1)S(1)}, bf16[2,256,256]{2,1,0:T(8,128)(2,1)S(1)}, u32[]{:S(2)}, u32[]{:S(2)}) collective-permute-start(bf16[2,256,256]{2,1,0:T(8,128)(2,1)S(1)} %bitcast.13), channel_id=1, source_target_pairs={{0,128},{8,393},{128,256},{136,8},{256,384},{264,136},{384,1},{392... | collective-permute-start | bytes 786440 | tf_op jit(solution)/shard_map/ppermute | solution.py:206
  11.3 17.3 %collective-permute-start = (bf16[256,256]{1,0:T(8,128)(2,1)}, bf16[256,256]{1,0:T(8,128)(2,1)S(1)}, u32[]{:S(2)}, u32[]{:S(2)}) collective-permute-start(bf16[256,256]{1,0:T(8,128)(2,1)} %points.1), channel_id=1, source_target_pairs={{0,256},{8,265},{128,384},{136,393},{256,1},{264,8},{384,129},{392... | collective-permute-start | bytes 393224 | tf_op jit(solution)/shard_map/ppermute | solution.py:206
  19.7 18.2 %all-to-all-start = ((f32[64,2,256]{2,1,0:T(2,128)}), f32[64,2,256]{2,1,0:T(2,128)S(1)}, u32[]{:S(2)}, u32[]{:S(2)}) async-start(f32[64,2,256]{2,1,0:T(2,128)} %first_pass.1), calls=%async_computation | async-start | bytes 262144 | tf_op jit(solution)/shard_map/all_to_all | solution.py:223

commit v5 on v4

--- a/solution.py
+++ b/solution.py
@@ -22,16 +22,15 @@
     return jnp.sum(wide * wide, axis=1, keepdims=True) * inv_temp
 
 
-def products(table, rows):
-    return lax.dot_general(
-        table,
-        rows * jnp.bfloat16(2.0 * inv_temp),
-        (((1,), (1,)), ((), ())),
-        preferred_element_type=jnp.float32,
-    )
-
-
-def first_kernel(centroids, points, stats, table, rows, arrived, ready):
+def columns(rows):
+    return (rows * jnp.bfloat16(2.0 * inv_temp)).T
+
+
+def products(table, columns):
+    return jnp.dot(table, columns, preferred_element_type=jnp.float32)
+
+
+def first_kernel(centroids, points, stats, reduced, table, rows, turned, arrived, ready):
     chunks = table.shape[0] // CHUNK
 
     def copy(i):
@@ -43,12 +42,13 @@
     for i in range(chunks):
         copy(i).start()
     own.wait()
+    turned[...] = columns(rows[...])
 
     def step(i, carry):
         peak, total = carry
         copy(i).wait()
         block = table[pl.ds(pl.multiple_of(i * CHUNK, CHUNK), CHUNK), :]
-        logits = products(block, rows[...]) - squares(block)
+        logits = products(block, turned[...]) - squares(block)
         top = jnp.maximum(peak, jnp.max(logits, axis=0, keepdims=True))
         total = total * jnp.exp(peak - top) + jnp.sum(jnp.exp(logits - top), axis=0, keepdims=True)
         return top, total
@@ -59,19 +59,28 @@
     both = jnp.concatenate([peak, total], axis=0)
     for i in range(stats.shape[0]):
         stats[i] = both
-
-
-def first_pass(points, centroids, receivers):
+    yl, co = (lax.axis_index(a) for a in GATHER)
+    count, owned, _ = reduced.shape
+    for z in range(count):
+        at = ((yl * count + z) * lax.axis_size("co") + co) * owned
+        reduced[z] = table[pl.ds(pl.multiple_of(at, owned), owned), :]
+
+
+def first_pass(points, centroids, receivers, reduced, owned):
     n, d = points.shape
     k = centroids.shape[0]
     return pl.pallas_call(
         first_kernel,
         in_specs=[pl.BlockSpec(memory_space=pltpu.HBM)] * 2,
-        out_specs=pl.BlockSpec(memory_space=pltpu.VMEM),
-        out_shape=jax.ShapeDtypeStruct((receivers, 2, n), jnp.float32),
+        out_specs=[pl.BlockSpec(memory_space=pltpu.VMEM)] * 2,
+        out_shape=[
+            jax.ShapeDtypeStruct((receivers, 2, n), jnp.float32),
+            jax.ShapeDtypeStruct((reduced, owned, d), centroids.dtype),
+        ],
         scratch_shapes=[
             pltpu.VMEM((k, d), centroids.dtype),
             pltpu.VMEM((n, d), points.dtype),
+            pltpu.VMEM((d, n), points.dtype),
             pltpu.SemaphoreType.DMA((k // CHUNK,)),
             pltpu.SemaphoreType.DMA,
         ],
@@ -101,7 +110,7 @@
     for at, (rows, off) in enumerate(pairs):
         for c in range(2):
             shift = log_norms[pl.ds(lax.rem(yl + off, 4) * 2 + c, 1), :]
-            logits = products(table[...], rows[c]) - norms
+            logits = products(table[...], columns(rows[c])) - norms
             shares = jnp.exp(logits - shift).astype(jnp.bfloat16)
             product = lax.dot_general(
                 shares, rows[c], (((1,), (0,)), ((), ())), preferred_element_type=jnp.float32
@@ -213,21 +222,13 @@
     reduced = lax.axis_size(REDUCE)
     owned = centroids.shape[0] // (gathered * reduced)
 
-    far = moved(points, (2, -2))
     near = lax.all_gather(points, "co")
-    side = moved(near, (1, -1))
-    stats = first_pass(points, centroids, cen * gathered)
-    far, side, _ = lax.optimization_barrier((far, side, stats))
+    side, far = moved(near, (1, -1)), moved(near, (2, -2))
+    stats, table = first_pass(points, centroids, cen * gathered, reduced, owned)
+    side, _ = lax.optimization_barrier((side, stats))
     sides = lax.all_gather(side, "co")
-    far = lax.all_gather(far, "co")
     every = lax.all_to_all(stats, (*CEN, *GATHER), 0, 0, tiled=True)
     every = every.reshape(cen, gathered, 2, n)
-    sizes = [lax.axis_size(a) for a in AXES]
-    at = (lax.axis_index("yl"), 0, lax.axis_index("co"), 0, 0)
-    table = lax.dynamic_slice(
-        centroids.reshape(*sizes, owned, d), at, (1, reduced, 1, owned, d)
-    )
-    table = lax.optimization_barrier(table.reshape(reduced, owned, d))
     parts, log_norm = second_pass(every, table, (near, sides, far))
     parts = lax.all_to_all(parts, REDUCE, 0, 0, tiled=True)
     return last_pass(parts, table), log_norm[0]

time: 69.9 us -> 69.8 us (level)
  waiting for transfers between devices: 4.99 us -> 8.09 us
  blocking collectives: 39.9 us -> 38 us
  local copies, waits for them, and re-layouts: 1.09 us -> 0 us
    all_to_all x1, waiting for transfers between devices: 4.99 us -> 8.09 us  [body(): every = lax.all_to_all(stats, (*CEN, *GATHER), 0, 0, tiled=True)]
    all_gather x1 -> x0, blocking collectives: 2.09 us -> none  [body(): far = lax.all_gather(far, 'co')]
    reshape x1 -> x0, local copies, waits for them, and re-layouts: 1.09 us -> none  [body(): table = lax.optimization_barrier(table.reshape(reduced, owned, d))]
  transfers between devices with their start and end apart: 3 -> 3, of which waited for: 1 -> 1; matrix products, arithmetic and copies ran while one was open for 2% -> 0% of each run, Pallas kernels for 9% -> 9%
where the time goes in v5:
time: 69.8 us; the launch traced here: 69.5 us
  blocking collectives  38 us (54%)
  starting transfers between devices  11.6 us (17%)
  Pallas kernels  11.2 us (16%)
  waiting for transfers between devices  8.09 us (12%)
    all_to_all x1, blocking collectives, body(): parts = lax.all_to_all(parts, REDUCE, 0, 0, tiled=True)  27 us
    all_gather x1, blocking collectives, body(): near = lax.all_gather(points, 'co')  8.72 us
    all_to_all x1, waiting for transfers between devices, body(): every = lax.all_to_all(stats, (*CEN, *GATHER), 0, 0, tiled=True)  8.09 us
    all_to_all x1, starting transfers between devices, body(): every = lax.all_to_all(stats, (*CEN, *GATHER), 0, 0, tiled=True)  7.78 us
    pallas_call x1, Pallas kernels, first_pass(): pl.pallas_call(first_kernel, in_specs=[pl.BlockSpec(memory_space=pltpu.HB...  6.48 us
    ppermute x2, starting transfers between devices, moved(): return lax.ppermute(array, RING, pairs)  3.83 us
    pallas_call x1, Pallas kernels, second_pass(): pl.pallas_call(second_kernel, in_specs=[pl.BlockSpec(memory_space=pltpu.V...  3.64 us
    all_gather x1, blocking collectives, body(): sides = lax.all_gather(side, 'co')  2.26 us
  transfers between devices with their start and end apart: 3, of which 1 were waited for; matrix products, arithmetic and copies ran while one was open for 0% of the time, Pallas kernels for 9%

profile of v5, /device:TPU:1, one launch (start us, length us, event | category | flops | bytes accessed | tf_op | source)
XLA Modules:
  0.0 69.5 jit_solution(13316467009536226972)
XLA Ops:
  0.6 8.7 %all-gather = bf16[512,256]{1,0:T(8,128)(2,1)S(1)} all-gather(bf16[256,256]{1,0:T(8,128)(2,1)} %points.1), channel_id=2, replica_groups=mesh['yl'=4,'z'=8,'co'=2,'x'=4,'yh'=2] {'co'}, dimensions={0}, use_global_device_ids=true | all-gather | bytes 393216 | tf_op jit(solution)/shard_map/all_gather | solution.py:225
  9.4 1.9 %collective-permute-start = (bf16[2,256,256]{2,1,0:T(8,128)(2,1)S(1)}, bf16[2,256,256]{2,1,0:T(8,128)(2,1)S(1)}, u32[]{:S(2)}, u32[]{:S(2)}) collective-permute-start(bf16[2,256,256]{2,1,0:T(8,128)(2,1)S(1)} %bitcast.7), channel_id=1, source_target_pairs={{0,128},{8,393},{128,256},{136,8},{256,384},{264,136},{384,1},{392... | collective-permute-start | bytes 786440 | tf_op jit(solution)/shard_map/ppermute | solution.py:215
  11.3 1.9 %collective-permute-start.1 = (bf16[2,256,256]{2,1,0:T(8,128)(2,1)S(1)}, bf16[2,256,256]{2,1,0:T(8,128)(2,1)S(1)}, u32[]{:S(2)}, u32[]{:S(2)}) collective-permute-start(bf16[2,256,256]{2,1,0:T(8,128)(2,1)S(1)} %bitcast.8), channel_id=1, source_target_pairs={{0,256},{8,265},{128,384},{136,393},{256,1},{264,8},{384,129},{392... | collective-permute-start | bytes 786440 | tf_op jit(solution)/shard_map/ppermute | solution.py:215
  13.2 6.5 %first_pass.1 = (f32[64,2,256]{2,1,0:T(2,128)}, bf16[8,128,256]{2,1,0:T(8,128)(2,1)S(1)}) custom-call(bf16[8192,256]{1,0:T(8,128)(2,1)} %centroids.1, bf16[256,256]{1,0:T(8,128)(2,1)} %points.1), custom_call_target="tpu_custom_call" | custom-call | flops 1073741824 | bytes 4194304 | tf_op jit(solution)/shard_map/first_pass/pallas_call | solution.py:72
  19.7 7.8 %all-to-all-start = ((f32[64,2,256]{2,1,0:T(2,128)}), f32[64,2,256]{2,1,0:T(2,128)S(1)}, u32[]{:S(2)}, u32[]{:S(2)}) async-start(f32[64,2,256]{2,1,0:T(2,128)} %get-tuple-element.7), calls=%async_computation | async-start | bytes 262144 | tf_op jit(solution)/shard_map/all_to_all | solution.py:230
  27.5 0.0 collective-permute-done
  27.5 2.3 %all-gather.1 = bf16[4,256,256]{2,1,0:T(8,128)(2,1)S(1)} all-gather(bf16[2,256,256]{2,1,0:T(8,128)(2,1)S(1)} %collective-permute-done), channel_id=3, replica_groups=mesh['yl'=4,'z'=8,'co'=2,'x'=4,'yh'=2] {'co'}, dimensions={0}, use_global_device_ids=true | all-gather | bytes 786432 | tf_op jit(solution)/shard_map/all_gather | solution.py:229
  29.8 8.1 %all-to-all-done = f32[64,2,256]{2,1,0:T(2,128)S(1)} async-done(((f32[64,2,256]{2,1,0:T(2,128)}), f32[64,2,256]{2,1,0:T(2,128)S(1)}, u32[]{:S(2)}, u32[]{:S(2)}) %all-to-all-start) | async-done | bytes 131104 | tf_op jit(solution)/shard_map/all_to_all | solution.py:230
  37.8 0.0 collective-permute-done.1.far
  37.8 3.6 %second_pass.1 = (bf16[8,144,256]{2,1,0:T(8,128)(2,1)S(1)}, f32[1,256]{1,0:T(1,128)}) custom-call(f32[8,8,2,256]{3,2,1,0:T(2,128)S(1)} %bitcast.10, bf16[1024,256]{1,0:T(8,128)(2,1)S(1)} %bitcast.6, bf16[2,256,256]{2,1,0:T(8,128)(2,1)S(1)} %bitcast.9, bf16[2,2,256,256]{3,2,1,0:T(8,128)(2,1)S(1)} %bitcast.5, bf16[2,256,256]{2,1,0:T(8,128)(2,1)S(1)} %collective-permute-done.1.far), custom_call_target="tpu_custom_call" | custom-call | flops 2147483648 | bytes 1048576 | tf_op jit(solution)/shard_map/second_pass/pallas_call | solution.py:152
  41.5 27.0 %all_to_all.10.parts = bf16[8,144,256]{2,1,0:T(8,128)(2,1)S(1)} all-to-all(bf16[8,144,256]{2,1,0:T(8,128)(2,1)S(1)} %get-tuple-element.10), channel_id=1, replica_groups=mesh['yl'=4,'z'=8,'co'=2,'x'=4,'yh'=2] {'z'}, dimensions={0} | all-to-all | bytes 1179648 | tf_op jit(solution)/shard_map/all_to_all | solution.py:233
  68.5 1.1 %last_pass.1 = f32[128,256]{1,0:T(8,128)} custom-call(bf16[8,144,256]{2,1,0:T(8,128)(2,1)S(1)} %all_to_all.10.parts, bf16[8,128,256]{2,1,0:T(8,128)(2,1)S(1)} %get-tuple-element.8.table), custom_call_target="tpu_custom_call" | custom-call | tf_op jit(solution)/shard_map/last_pass/pallas_call | solution.py:193
Async XLA Ops:
  9.4 18.1 %collective-permute-start = (bf16[2,256,256]{2,1,0:T(8,128)(2,1)S(1)}, bf16[2,256,256]{2,1,0:T(8,128)(2,1)S(1)}, u32[]{:S(2)}, u32[]{:S(2)}) collective-permute-start(bf16[2,256,256]{2,1,0:T(8,128)(2,1)S(1)} %bitcast.7), channel_id=1, source_target_pairs={{0,128},{8,393},{128,256},{136,8},{256,384},{264,136},{384,1},{392... | collective-permute-start | bytes 786440 | tf_op jit(solution)/shard_map/ppermute | solution.py:215
  11.3 26.6 %collective-permute-start.1 = (bf16[2,256,256]{2,1,0:T(8,128)(2,1)S(1)}, bf16[2,256,256]{2,1,0:T(8,128)(2,1)S(1)}, u32[]{:S(2)}, u32[]{:S(2)}) collective-permute-start(bf16[2,256,256]{2,1,0:T(8,128)(2,1)S(1)} %bitcast.8), channel_id=1, source_target_pairs={{0,256},{8,265},{128,384},{136,393},{256,1},{264,8},{384,129},{392... | collective-permute-start | bytes 786440 | tf_op jit(solution)/shard_map/ppermute | solution.py:215
  19.7 18.1 %all-to-all-start = ((f32[64,2,256]{2,1,0:T(2,128)}), f32[64,2,256]{2,1,0:T(2,128)S(1)}, u32[]{:S(2)}, u32[]{:S(2)}) async-start(f32[64,2,256]{2,1,0:T(2,128)} %get-tuple-element.7), calls=%async_computation | async-start | bytes 262144 | tf_op jit(solution)/shard_map/all_to_all | solution.py:230

commit v6 on v5

--- a/solution.py
+++ b/solution.py
@@ -106,26 +106,26 @@
     own_norm[...] = log_norms[pl.ds(yl * 2 + co, 1), :]
 
     norms = squares(table[...])
+    cores, n, d = near.shape
     pairs = ((near, 0), (sides.at[0], 3), (sides.at[1], 1), (far, 2))
     for at, (rows, off) in enumerate(pairs):
-        for c in range(2):
-            shift = log_norms[pl.ds(lax.rem(yl + off, 4) * 2 + c, 1), :]
-            logits = products(table[...], columns(rows[c])) - norms
-            shares = jnp.exp(logits - shift).astype(jnp.bfloat16)
-            product = lax.dot_general(
-                shares, rows[c], (((1,), (0,)), ((), ())), preferred_element_type=jnp.float32
-            )
-            wide = shares.astype(jnp.float32)
-            mass = wide[:, :128] + wide[:, 128:]
-            if at == 0 and c == 0:
-                sums[...] = product
-                masses[...] = mass
-            else:
-                sums[...] += product
-                masses[...] += mass
-
-    owned, d = parts.shape[1] - 16, parts.shape[2]
-    line = lax.broadcasted_iota(jnp.int32, (16, d), 0)
+        chip = lax.rem(yl + off, 4) * cores
+        shift = [log_norms[pl.ds(chip + c, 1), :] for c in range(cores)]
+        pair = rows[...].reshape(cores * n, d)
+        logits = products(table[...], columns(pair)) - norms
+        shares = jnp.exp(logits - jnp.concatenate(shift, axis=1)).astype(jnp.bfloat16)
+        product = jnp.dot(shares, pair, preferred_element_type=jnp.float32)
+        wide = shares.astype(jnp.float32)
+        mass = sum(wide[:, i : i + 128] for i in range(0, cores * n, 128))
+        if at == 0:
+            sums[...] = product
+            masses[...] = mass
+        else:
+            sums[...] += product
+            masses[...] += mass
+
+    owned = sums.shape[0] // parts.shape[0]
+    line = lax.broadcasted_iota(jnp.int32, (16, 128), 0)
     for r in range(parts.shape[0]):
         here = slice(r * owned, (r + 1) * owned)
         mass = masses[here, :]
@@ -134,15 +134,16 @@
         scale = jnp.maximum(jnp.max(size, axis=0, keepdims=True) * 1.01, 1e-30)
         scale = scale.astype(jnp.bfloat16).astype(jnp.float32)
         code = jnp.exp2(size * (SPAN / scale) - FLOOR)
-        parts[r, :owned, :] = jnp.where(mean < 0.0, -code, code).astype(jnp.bfloat16)
+        code = jnp.where(mean < 0.0, -code, code).astype(jnp.bfloat16)
+        parts[r, :owned, :] = code[:, :128]
+        parts[r, owned : 2 * owned, :] = code[:, 128:]
         mass = jnp.sum(mass.T, axis=0, keepdims=True)
         high = mass.astype(jnp.bfloat16).astype(jnp.float32)
         mid = (mass - high).astype(jnp.bfloat16).astype(jnp.float32)
-        low = mass - high - mid
-        upper = jnp.concatenate([high, mid], axis=1)
-        lower = jnp.concatenate([low, jnp.zeros_like(low)], axis=1)
-        tail = jnp.where(line == 0, scale, jnp.where(line == 1, upper, lower))
-        parts[r, owned:, :] = tail.astype(jnp.bfloat16)
+        tail = mass - high - mid
+        for at, row in enumerate((scale[:, :128], scale[:, 128:], high, mid)):
+            tail = jnp.where(line == at, row, tail)
+        parts[r, 2 * owned :, :] = tail.astype(jnp.bfloat16)
 
 
 def second_pass(stats, table, blocks):
@@ -154,7 +155,7 @@
         in_specs=[pl.BlockSpec(memory_space=pltpu.VMEM)] * 5,
         out_specs=[pl.BlockSpec(memory_space=pltpu.VMEM)] * 2,
         out_shape=[
-            jax.ShapeDtypeStruct((reduced, owned + 16, d), jnp.bfloat16),
+            jax.ShapeDtypeStruct((reduced, 2 * owned + 16, d // 2), jnp.bfloat16),
             jax.ShapeDtypeStruct((1, n), jnp.float32),
         ],
         scratch_shapes=[
@@ -176,14 +177,14 @@
     sums = own.astype(jnp.float32)
     masses = jnp.ones((owned, owned), jnp.float32)
     for r in range(parts.shape[0]):
-        tail = parts[r, owned:, :].astype(jnp.float32)
-        mass = tail[1:2, :owned] + tail[1:2, owned:] + tail[2:3, :owned]
-        mass = jnp.broadcast_to(mass, (owned, owned)).T
-        code = parts[r, :owned, :].astype(jnp.float32)
-        size = (jnp.log2(jnp.abs(code)) + FLOOR) * (tail[0:1, :] / SPAN)
-        mean = jnp.where(code < 0.0, -size, size)
-        weight = 1.0 + mass
-        sums = sums + mean * jnp.concatenate([weight, weight], axis=1)
+        tail = parts[r, 2 * owned :, :].astype(jnp.float32)
+        mass = jnp.broadcast_to(tail[2:3] + tail[3:4] + tail[4:5], (owned, owned)).T
+        means = []
+        for half in range(2):
+            code = parts[r, half * owned : (half + 1) * owned, :].astype(jnp.float32)
+            size = (jnp.log2(jnp.abs(code)) + FLOOR) * (tail[half : half + 1] / SPAN)
+            means.append(jnp.where(code < 0.0, -size, size) * (1.0 + mass))
+        sums = sums + jnp.concatenate(means, axis=1)
         masses = masses + mass
     updated[...] = sums / jnp.concatenate([masses, masses], axis=1)
 

time: 69.8 us -> 69 us (0.989)
  blocking collectives: 38 us -> 37.3 us
where the time goes in v6:
time: 69 us; the launch traced here: 68.8 us
  blocking collectives  37.3 us (54%)
  starting transfers between devices  11.6 us (17%)
  Pallas kernels  11.1 us (16%)
  waiting for transfers between devices  8.09 us (12%)
    all_to_all x1, blocking collectives, body(): parts = lax.all_to_all(parts, REDUCE, 0, 0, tiled=True)  26.3 us
    all_gather x1, blocking collectives, body(): near = lax.all_gather(points, 'co')  8.72 us
    all_to_all x1, waiting for transfers between devices, body(): every = lax.all_to_all(stats, (*CEN, *GATHER), 0, 0, tiled=True)  8.09 us
    all_to_all x1, starting transfers between devices, body(): every = lax.all_to_all(stats, (*CEN, *GATHER), 0, 0, tiled=True)  7.78 us
    pallas_call x1, Pallas kernels, first_pass(): pl.pallas_call(first_kernel, in_specs=[pl.BlockSpec(memory_space=pltpu.HB...  6.48 us
    ppermute x2, starting transfers between devices, moved(): return lax.ppermute(array, RING, pairs)  3.83 us
    pallas_call x1, Pallas kernels, second_pass(): pl.pallas_call(second_kernel, in_specs=[pl.BlockSpec(memory_space=pltpu.V...  3.55 us
    all_gather x1, blocking collectives, body(): sides = lax.all_gather(side, 'co')  2.26 us
  transfers between devices with their start and end apart: 3, of which 1 were waited for; matrix products, arithmetic and copies ran while one was open for 0% of the time, Pallas kernels for 9%

profile of v6, /device:TPU:1, one launch (start us, length us, event | category | flops | bytes accessed | tf_op | source)
XLA Modules:
  0.0 68.8 jit_solution(8662992601788900653)
XLA Ops:
  0.6 8.7 %all-gather = bf16[512,256]{1,0:T(8,128)(2,1)S(1)} all-gather(bf16[256,256]{1,0:T(8,128)(2,1)} %points.1), channel_id=2, replica_groups=mesh['yl'=4,'z'=8,'co'=2,'x'=4,'yh'=2] {'co'}, dimensions={0}, use_global_device_ids=true | all-gather | bytes 393216 | tf_op jit(solution)/shard_map/all_gather | solution.py:226
  9.4 1.9 %collective-permute-start = (bf16[2,256,256]{2,1,0:T(8,128)(2,1)S(1)}, bf16[2,256,256]{2,1,0:T(8,128)(2,1)S(1)}, u32[]{:S(2)}, u32[]{:S(2)}) collective-permute-start(bf16[2,256,256]{2,1,0:T(8,128)(2,1)S(1)} %bitcast.7), channel_id=1, source_target_pairs={{0,128},{8,393},{128,256},{136,8},{256,384},{264,136},{384,1},{392... | collective-permute-start | bytes 786440 | tf_op jit(solution)/shard_map/ppermute | solution.py:216
  11.3 1.9 %collective-permute-start.1 = (bf16[2,256,256]{2,1,0:T(8,128)(2,1)S(1)}, bf16[2,256,256]{2,1,0:T(8,128)(2,1)S(1)}, u32[]{:S(2)}, u32[]{:S(2)}) collective-permute-start(bf16[2,256,256]{2,1,0:T(8,128)(2,1)S(1)} %bitcast.8), channel_id=1, source_target_pairs={{0,256},{8,265},{128,384},{136,393},{256,1},{264,8},{384,129},{392... | collective-permute-start | bytes 786440 | tf_op jit(solution)/shard_map/ppermute | solution.py:216
  13.2 6.5 %first_pass.1 = (f32[64,2,256]{2,1,0:T(2,128)}, bf16[8,128,256]{2,1,0:T(8,128)(2,1)S(1)}) custom-call(bf16[8192,256]{1,0:T(8,128)(2,1)} %centroids.1, bf16[256,256]{1,0:T(8,128)(2,1)} %points.1), custom_call_target="tpu_custom_call" | custom-call | flops 1073741824 | bytes 4194304 | tf_op jit(solution)/shard_map/first_pass/pallas_call | solution.py:72
  19.7 7.8 %all-to-all-start = ((f32[64,2,256]{2,1,0:T(2,128)}), f32[64,2,256]{2,1,0:T(2,128)S(1)}, u32[]{:S(2)}, u32[]{:S(2)}) async-start(f32[64,2,256]{2,1,0:T(2,128)} %get-tuple-element.7), calls=%async_computation | async-start | bytes 262144 | tf_op jit(solution)/shard_map/all_to_all | solution.py:231
  27.5 0.0 collective-permute-done
  27.5 2.3 %all-gather.1 = bf16[4,256,256]{2,1,0:T(8,128)(2,1)S(1)} all-gather(bf16[2,256,256]{2,1,0:T(8,128)(2,1)S(1)} %collective-permute-done), channel_id=3, replica_groups=mesh['yl'=4,'z'=8,'co'=2,'x'=4,'yh'=2] {'co'}, dimensions={0}, use_global_device_ids=true | all-gather | bytes 786432 | tf_op jit(solution)/shard_map/all_gather | solution.py:230
  29.8 8.1 %all-to-all-done = f32[64,2,256]{2,1,0:T(2,128)S(1)} async-done(((f32[64,2,256]{2,1,0:T(2,128)}), f32[64,2,256]{2,1,0:T(2,128)S(1)}, u32[]{:S(2)}, u32[]{:S(2)}) %all-to-all-start) | async-done | bytes 131104 | tf_op jit(solution)/shard_map/all_to_all | solution.py:231
  37.8 0.0 collective-permute-done.1.far
  37.8 3.5 %second_pass.1 = (bf16[8,272,128]{2,1,0:T(8,128)(2,1)S(1)}, f32[1,256]{1,0:T(1,128)}) custom-call(f32[8,8,2,256]{3,2,1,0:T(2,128)S(1)} %bitcast.10, bf16[1024,256]{1,0:T(8,128)(2,1)S(1)} %bitcast.5, bf16[2,256,256]{2,1,0:T(8,128)(2,1)S(1)} %bitcast.9, bf16[2,2,256,256]{3,2,1,0:T(8,128)(2,1)S(1)} %bitcast.6, bf16[2,256,256]{2,1,0:T(8,128)(2,1)S(1)} %collective-permute-done.1.far), custom_call_target="tpu_custom_call" | custom-call | flops 2147483648 | bytes 1048576 | tf_op jit(solution)/shard_map/second_pass/pallas_call | solution.py:153
  41.4 26.3 %all_to_all.10.parts = bf16[8,272,128]{2,1,0:T(8,128)(2,1)S(1)} all-to-all(bf16[8,272,128]{2,1,0:T(8,128)(2,1)S(1)} %get-tuple-element.10), channel_id=1, replica_groups=mesh['yl'=4,'z'=8,'co'=2,'x'=4,'yh'=2] {'z'}, dimensions={0} | all-to-all | bytes 1114112 | tf_op jit(solution)/shard_map/all_to_all | solution.py:234
  67.7 1.1 %last_pass.1 = f32[128,256]{1,0:T(8,128)} custom-call(bf16[8,272,128]{2,1,0:T(8,128)(2,1)S(1)} %all_to_all.10.parts, bf16[8,128,256]{2,1,0:T(8,128)(2,1)S(1)} %get-tuple-element.8.table), custom_call_target="tpu_custom_call" | custom-call | tf_op jit(solution)/shard_map/last_pass/pallas_call | solution.py:194
Async XLA Ops:
  9.4 18.1 %collective-permute-start = (bf16[2,256,256]{2,1,0:T(8,128)(2,1)S(1)}, bf16[2,256,256]{2,1,0:T(8,128)(2,1)S(1)}, u32[]{:S(2)}, u32[]{:S(2)}) collective-permute-start(bf16[2,256,256]{2,1,0:T(8,128)(2,1)S(1)} %bitcast.7), channel_id=1, source_target_pairs={{0,128},{8,393},{128,256},{136,8},{256,384},{264,136},{384,1},{392... | collective-permute-start | bytes 786440 | tf_op jit(solution)/shard_map/ppermute | solution.py:216
  11.3 26.6 %collective-permute-start.1 = (bf16[2,256,256]{2,1,0:T(8,128)(2,1)S(1)}, bf16[2,256,256]{2,1,0:T(8,128)(2,1)S(1)}, u32[]{:S(2)}, u32[]{:S(2)}) collective-permute-start(bf16[2,256,256]{2,1,0:T(8,128)(2,1)S(1)} %bitcast.8), channel_id=1, source_target_pairs={{0,256},{8,265},{128,384},{136,393},{256,1},{264,8},{384,129},{392... | collective-permute-start | bytes 786440 | tf_op jit(solution)/shard_map/ppermute | solution.py:216
  19.7 18.1 %all-to-all-start = ((f32[64,2,256]{2,1,0:T(2,128)}), f32[64,2,256]{2,1,0:T(2,128)S(1)}, u32[]{:S(2)}, u32[]{:S(2)}) async-start(f32[64,2,256]{2,1,0:T(2,128)} %get-tuple-element.7), calls=%async_computation | async-start | bytes 262144 | tf_op jit(solution)/shard_map/all_to_all | solution.py:231

commit v7 on v6

--- a/solution.py
+++ b/solution.py
@@ -6,11 +6,11 @@
 from jax.sharding import Mesh
 from jax.sharding import PartitionSpec as P
 
-AXES = ("yl", "z", "co")
+AXES = ("ya", "yb", "za", "zb", "co")
 CEN = ("x", "yh")
-GATHER = ("yl", "co")
-REDUCE = "z"
-RING = ("yl", "co", "yh")
+SQUARE = ("yb", "zb")
+GATHER = ("yb", "zb", "co")
+REDUCE = ("ya", "za")
 MIB = 1 << 20
 CHUNK = 2048
 inv_temp = 0.0625
@@ -59,11 +59,14 @@
     both = jnp.concatenate([peak, total], axis=0)
     for i in range(stats.shape[0]):
         stats[i] = both
-    yl, co = (lax.axis_index(a) for a in GATHER)
-    count, owned, _ = reduced.shape
-    for z in range(count):
-        at = ((yl * count + z) * lax.axis_size("co") + co) * owned
-        reduced[z] = table[pl.ds(pl.multiple_of(at, owned), owned), :]
+    owned = reduced.shape[1]
+    place = {a: lax.axis_index(a) for a in AXES}
+    for r in range(reduced.shape[0]):
+        place["ya"], place["za"] = divmod(r, lax.axis_size("za"))
+        at = 0
+        for a in AXES:
+            at = at * lax.axis_size(a) + place[a]
+        reduced[r] = table[pl.ds(pl.multiple_of(at * owned, owned), owned), :]
 
 
 def first_pass(points, centroids, receivers, reduced, owned):
@@ -92,8 +95,8 @@
     )(*(pltpu.with_memory_space_constraint(a, pltpu.HBM) for a in (centroids, points)))
 
 
-def second_kernel(stats, table, near, sides, far, parts, own_norm, log_norms, sums, masses):
-    yl, co = (lax.axis_index(a) for a in GATHER)
+def second_kernel(stats, table, here, there, parts, own_norm, log_norms, sums, masses):
+    co = lax.axis_index("co")
 
     cen = stats.shape[0]
     peak = stats[0, :, 0, :]
@@ -103,21 +106,20 @@
     for c in range(1, cen):
         total = total + stats[c, :, 1, :] * jnp.exp(stats[c, :, 0, :] - peak)
     log_norms[...] = peak + jnp.log(total)
-    own_norm[...] = log_norms[pl.ds(yl * 2 + co, 1), :]
+    own_norm[...] = log_norms[pl.ds(lax.axis_index(SQUARE) * 2 + co, 1), :]
 
     norms = squares(table[...])
-    cores, n, d = near.shape
-    pairs = ((near, 0), (sides.at[0], 3), (sides.at[1], 1), (far, 2))
-    for at, (rows, off) in enumerate(pairs):
-        chip = lax.rem(yl + off, 4) * cores
-        shift = [log_norms[pl.ds(chip + c, 1), :] for c in range(cores)]
-        pair = rows[...].reshape(cores * n, d)
+    chips, n, d = here.shape
+    pairs = [(rows, core, at) for rows, core in ((here, co), (there, 1 - co)) for at in (0, 2)]
+    for rows, core, at in pairs:
+        shift = [log_norms[pl.ds((at + i) * 2 + core, 1), :] for i in range(2)]
+        pair = rows[at : at + 2].reshape(2 * n, d)
         logits = products(table[...], columns(pair)) - norms
         shares = jnp.exp(logits - jnp.concatenate(shift, axis=1)).astype(jnp.bfloat16)
         product = jnp.dot(shares, pair, preferred_element_type=jnp.float32)
         wide = shares.astype(jnp.float32)
-        mass = sum(wide[:, i : i + 128] for i in range(0, cores * n, 128))
-        if at == 0:
+        mass = sum(wide[:, i : i + 128] for i in range(0, 2 * n, 128))
+        if rows is here and at == 0:
             sums[...] = product
             masses[...] = mass
         else:
@@ -152,7 +154,7 @@
     k = owned * reduced
     return pl.pallas_call(
         second_kernel,
-        in_specs=[pl.BlockSpec(memory_space=pltpu.VMEM)] * 5,
+        in_specs=[pl.BlockSpec(memory_space=pltpu.VMEM)] * 4,
         out_specs=[pl.BlockSpec(memory_space=pltpu.VMEM)] * 2,
         out_shape=[
             jax.ShapeDtypeStruct((reduced, 2 * owned + 16, d // 2), jnp.bfloat16),
@@ -201,21 +203,6 @@
     )(parts, table)
 
 
-def moved(array, hops):
-    low, cores, high = (lax.axis_size(a) for a in RING)
-    ring = low * high
-
-    def place(y, core):
-        return ((y % low) * cores + core) * high + y // low
-
-    pairs = [
-        (place(y, core), place((y + hops[core]) % ring, core))
-        for y in range(ring)
-        for core in range(cores)
-    ]
-    return lax.ppermute(array, RING, pairs)
-
-
 def body(points, centroids):
     n, d = points.shape
     cen = lax.axis_size(CEN)
@@ -223,20 +210,20 @@
     reduced = lax.axis_size(REDUCE)
     owned = centroids.shape[0] // (gathered * reduced)
 
-    near = lax.all_gather(points, "co")
-    side, far = moved(near, (1, -1)), moved(near, (2, -2))
+    copies = jnp.broadcast_to(points, (lax.axis_size(SQUARE), n, d))
+    here = lax.all_to_all(copies, SQUARE, 0, 0, tiled=True)
     stats, table = first_pass(points, centroids, cen * gathered, reduced, owned)
-    side, _ = lax.optimization_barrier((side, stats))
-    sides = lax.all_gather(side, "co")
+    after, _ = lax.optimization_barrier((here, stats))
+    there = lax.ppermute(after, "co", [(0, 1), (1, 0)])
     every = lax.all_to_all(stats, (*CEN, *GATHER), 0, 0, tiled=True)
     every = every.reshape(cen, gathered, 2, n)
-    parts, log_norm = second_pass(every, table, (near, sides, far))
+    parts, log_norm = second_pass(every, table, (here, there))
     parts = lax.all_to_all(parts, REDUCE, 0, 0, tiled=True)
     return last_pass(parts, table), log_norm[0]
 
 
 def solution(mesh):
-    torus = Mesh(mesh.devices.reshape(4, 8, 2, 4, 2), (*AXES, *CEN))
+    torus = Mesh(mesh.devices.reshape(2, 2, 4, 2, 2, 4, 2), (*AXES, *CEN))
     in_specs = (P(AXES, None), P(CEN, None))
     out_specs = (P((*CEN, *AXES), None), P(AXES))
     return jax.shard_map(body, mesh=torus, in_specs=in_specs, out_specs=out_specs, check_vma=False)

time: 69 us -> 73.1 us (1.059)
  blocking collectives: 37.3 us -> 47 us
  waiting for transfers between devices: 8.09 us -> 0.01 us
  local copies, waits for them, and re-layouts: 0 us -> 1.74 us
  starting transfers between devices: 11.6 us -> 12.9 us
    all_to_all x0 -> x1, blocking collectives: none -> 18.1 us  [body(): every = lax.all_to_all(stats, (*CEN, *GATHER), 0, 0, tiled=True)]
    all_gather x2 -> x0, blocking collectives: 11 us -> none  [the longest x1 8.72 us: body(): near = lax.all_gather(points, 'co')]
    all_to_all x1, waiting for transfers between devices: 8.09 us -> 0.01 us  [body(): here = lax.all_to_all(copies, SQUARE, 0, 0, tiled=True)]
    ppermute x2 -> x1, starting transfers between devices: 3.83 us -> 7.72 us  [body(): there = lax.ppermute(after, 'co', [(0, 1), (1, 0)])]
    all_to_all x1, blocking collectives: 26.3 us -> 28.9 us  [body(): parts = lax.all_to_all(parts, REDUCE, 0, 0, tiled=True)]
    all_to_all x1, starting transfers between devices: 7.78 us -> 5.2 us  [body(): here = lax.all_to_all(copies, SQUARE, 0, 0, tiled=True)]
    broadcast_in_dim x0 -> x1, local copies, waits for them, and re-layouts: none -> 1.74 us  [body(): copies = jnp.broadcast_to(points, (lax.axis_size(SQUARE), n, d))]
  transfers between devices with their start and end apart: 3 -> 2, of which waited for: 1 -> 0; matrix products, arithmetic and copies ran while one was open for 0% -> 0% of each run, Pallas kernels for 9% -> 8%
where the time goes in v7:
time: 73.1 us; the launch traced here: 72.8 us
  blocking collectives  47 us (64%)
  starting transfers between devices  12.9 us (18%)
  Pallas kernels  10.5 us (14%)
  local copies, waits for them, and re-layouts  1.74 us (2%)
    all_to_all x1, blocking collectives, body(): parts = lax.all_to_all(parts, REDUCE, 0, 0, tiled=True)  28.9 us
    all_to_all x1, blocking collectives, body(): every = lax.all_to_all(stats, (*CEN, *GATHER), 0, 0, tiled=True)  18.1 us
    ppermute x1, starting transfers between devices, body(): there = lax.ppermute(after, 'co', [(0, 1), (1, 0)])  7.72 us
    pallas_call x1, Pallas kernels, first_pass(): pl.pallas_call(first_kernel, in_specs=[pl.BlockSpec(memory_space=pltpu.HB...  5.86 us
    all_to_all x1, starting transfers between devices, body(): here = lax.all_to_all(copies, SQUARE, 0, 0, tiled=True)  5.2 us
    pallas_call x1, Pallas kernels, second_pass(): pl.pallas_call(second_kernel, in_specs=[pl.BlockSpec(memory_space=pltpu.V...  3.55 us
    broadcast_in_dim x1, local copies, waits for them, and re-layouts, body(): copies = jnp.broadcast_to(points, (lax.axis_size(SQUARE), n, d))  1.74 us
  transfers between devices with their start and end apart: 2, of which 0 were waited for; matrix products, arithmetic and copies ran while one was open for 0% of the time, Pallas kernels for 8%

profile of v7, /device:TPU:1, one launch (start us, length us, event | category | flops | bytes accessed | tf_op | source)
XLA Modules:
  0.0 72.8 jit_solution(9572538972431797377)
XLA Ops:
  0.6 1.7 %broadcast_in_dim.3 = bf16[4,256,256]{2,1,0:T(8,128)(2,1)} broadcast(bf16[256,256]{1,0:T(8,128)(2,1)} %points.1), dimensions={1,2} | broadcast | bytes 655360 | tf_op jit(solution)/shard_map/broadcast_in_dim | solution.py:213
  2.4 5.2 %all-to-all-start.1 = ((bf16[4,256,256]{2,1,0:T(8,128)(2,1)}), bf16[4,256,256]{2,1,0:T(8,128)(2,1)S(1)}, u32[]{:S(2)}, u32[]{:S(2)}) async-start(bf16[4,256,256]{2,1,0:T(8,128)(2,1)} %broadcast_in_dim.3), calls=%async_computation.1 | async-start | bytes 1048576 | tf_op jit(solution)/shard_map/all_to_all | solution.py:214
  7.6 5.9 %first_pass.1 = (f32[64,2,256]{2,1,0:T(2,128)S(1)}, bf16[8,128,256]{2,1,0:T(8,128)(2,1)S(1)}) custom-call(bf16[8192,256]{1,0:T(8,128)(2,1)} %centroids.1, bf16[256,256]{1,0:T(8,128)(2,1)} %points.1), custom_call_target="tpu_custom_call" | custom-call | flops 1073741824 | bytes 4194304 | tf_op jit(solution)/shard_map/first_pass/pallas_call | solution.py:75
  13.4 0.0 all-to-all-done.1.here
  13.4 7.7 %collective-permute-start = (bf16[4,256,256]{2,1,0:T(8,128)(2,1)S(1)}, bf16[4,256,256]{2,1,0:T(8,128)(2,1)S(1)}, u32[]{:S(2)}, u32[]{:S(2)}) collective-permute-start(bf16[4,256,256]{2,1,0:T(8,128)(2,1)S(1)} %all-to-all-done.1.here), channel_id=1, source_target_pairs={{0,8},{8,0},{1,9},{9,1},{2,10},{10,2},{3,11},{11,3},{4,12},{12,4},... | collective-permute-start | bytes 1572872 | tf_op jit(solution)/shard_map/ppermute | solution.py:217
  21.2 18.1 %all_to_all.15 = f32[64,2,256]{2,1,0:T(2,128)S(1)} all-to-all(f32[64,2,256]{2,1,0:T(2,128)S(1)} %get-tuple-element.7), channel_id=1, replica_groups=mesh['ya'=2,'yb'=2,'za'=4,'zb'=2,'co'=2,'x'=4,'yh'=2] {'x','yh','yb','zb..., dimensions={0} | all-to-all | bytes 262144 | tf_op jit(solution)/shard_map/all_to_all | solution.py:218
  39.3 0.0 collective-permute-done.there
  39.3 3.5 %second_pass.1 = (bf16[8,272,128]{2,1,0:T(8,128)(2,1)S(1)}, f32[1,256]{1,0:T(1,128)}) custom-call(f32[8,8,2,256]{3,2,1,0:T(2,128)S(1)} %bitcast.4, bf16[1024,256]{1,0:T(8,128)(2,1)S(1)} %bitcast.3, bf16[4,256,256]{2,1,0:T(8,128)(2,1)S(1)} %all-to-all-done.1.here, bf16[4,256,256]{2,1,0:T(8,128)(2,1)S(1)} %collective-permute-done.there), custom_call_target="tpu_custom_call" | custom-call | flops 2147483648 | bytes 1048576 | tf_op jit(solution)/shard_map/second_pass/pallas_call | solution.py:155
  42.8 28.9 %all_to_all.16.parts = bf16[8,272,128]{2,1,0:T(8,128)(2,1)S(1)} all-to-all(bf16[8,272,128]{2,1,0:T(8,128)(2,1)S(1)} %get-tuple-element.10), channel_id=1, replica_groups=mesh['ya'=2,'yb'=2,'za'=4,'zb'=2,'co'=2,'x'=4,'yh'=2] {'ya','za'}, dimensions={0} | all-to-all | bytes 1114112 | tf_op jit(solution)/shard_map/all_to_all | solution.py:221
  71.7 1.1 %last_pass.1 = f32[128,256]{1,0:T(8,128)} custom-call(bf16[8,272,128]{2,1,0:T(8,128)(2,1)S(1)} %all_to_all.16.parts, bf16[8,128,256]{2,1,0:T(8,128)(2,1)S(1)} %get-tuple-element.8.table), custom_call_target="tpu_custom_call" | custom-call | tf_op jit(solution)/shard_map/last_pass/pallas_call | solution.py:196
Async XLA Ops:
  2.4 11.1 %all-to-all-start.1 = ((bf16[4,256,256]{2,1,0:T(8,128)(2,1)}), bf16[4,256,256]{2,1,0:T(8,128)(2,1)S(1)}, u32[]{:S(2)}, u32[]{:S(2)}) async-start(bf16[4,256,256]{2,1,0:T(8,128)(2,1)} %broadcast_in_dim.3), calls=%async_computation.1 | async-start | bytes 1048576 | tf_op jit(solution)/shard_map/all_to_all | solution.py:214
  13.4 25.8 %collective-permute-start = (bf16[4,256,256]{2,1,0:T(8,128)(2,1)S(1)}, bf16[4,256,256]{2,1,0:T(8,128)(2,1)S(1)}, u32[]{:S(2)}, u32[]{:S(2)}) collective-permute-start(bf16[4,256,256]{2,1,0:T(8,128)(2,1)S(1)} %all-to-all-done.1.here), channel_id=1, source_target_pairs={{0,8},{8,0},{1,9},{9,1},{2,10},{10,2},{3,11},{11,3},{4,12},{12,4},... | collective-permute-start | bytes 1572872 | tf_op jit(solution)/shard_map/ppermute | solution.py:217

commit v8 on v6

--- a/solution.py
+++ b/solution.py
@@ -31,31 +31,27 @@
 
 
 def first_kernel(centroids, points, stats, reduced, table, rows, turned, arrived, ready):
-    chunks = table.shape[0] // CHUNK
-
-    def copy(i):
-        here = pl.ds(i * CHUNK, CHUNK)
-        return pltpu.make_async_copy(centroids.at[here], table.at[here], arrived.at[i])
-
+    pieces = (slice(0, CHUNK), slice(CHUNK, table.shape[0]))
     own = pltpu.make_async_copy(points, rows, ready)
+    copies = [
+        pltpu.make_async_copy(centroids.at[piece], table.at[piece], arrived.at[i])
+        for i, piece in enumerate(pieces)
+    ]
     own.start()
-    for i in range(chunks):
-        copy(i).start()
+    for copy in copies:
+        copy.start()
     own.wait()
     turned[...] = columns(rows[...])
 
-    def step(i, carry):
-        peak, total = carry
-        copy(i).wait()
-        block = table[pl.ds(pl.multiple_of(i * CHUNK, CHUNK), CHUNK), :]
+    found = []
+    for copy, piece in zip(copies, pieces):
+        copy.wait()
+        block = table[piece, :]
         logits = products(block, turned[...]) - squares(block)
-        top = jnp.maximum(peak, jnp.max(logits, axis=0, keepdims=True))
-        total = total * jnp.exp(peak - top) + jnp.sum(jnp.exp(logits - top), axis=0, keepdims=True)
-        return top, total
-
-    n = rows.shape[0]
-    start = (jnp.full((1, n), -jnp.inf, jnp.float32), jnp.zeros((1, n), jnp.float32))
-    peak, total = lax.fori_loop(0, chunks, step, start)
+        top = jnp.max(logits, axis=0, keepdims=True)
+        found.append((top, jnp.sum(jnp.exp(logits - top), axis=0, keepdims=True)))
+    peak = jnp.maximum(found[0][0], found[1][0])
+    total = sum(part * jnp.exp(top - peak) for top, part in found)
     both = jnp.concatenate([peak, total], axis=0)
     for i in range(stats.shape[0]):
         stats[i] = both
@@ -81,10 +77,10 @@
             pltpu.VMEM((k, d), centroids.dtype),
             pltpu.VMEM((n, d), points.dtype),
             pltpu.VMEM((d, n), points.dtype),
-            pltpu.SemaphoreType.DMA((k // CHUNK,)),
+            pltpu.SemaphoreType.DMA((2,)),
             pltpu.SemaphoreType.DMA,
         ],
-        compiler_params=pltpu.CompilerParams(vmem_limit_bytes=24 * MIB),
+        compiler_params=pltpu.CompilerParams(vmem_limit_bytes=32 * MIB),
         cost_estimate=pl.CostEstimate(
             flops=2 * n * k * d, bytes_accessed=2 * k * d, transcendentals=n * k
         ),
@@ -107,17 +103,18 @@
 
     norms = squares(table[...])
     cores, n, d = near.shape
-    pairs = ((near, 0), (sides.at[0], 3), (sides.at[1], 1), (far, 2))
-    for at, (rows, off) in enumerate(pairs):
-        chip = lax.rem(yl + off, 4) * cores
-        shift = [log_norms[pl.ds(chip + c, 1), :] for c in range(cores)]
-        pair = rows[...].reshape(cores * n, d)
-        logits = products(table[...], columns(pair)) - norms
+    groups = ((near, (0,)), (sides, (3, 1)), (far, (2,)))
+    for rows, offs in groups:
+        chips = [lax.rem(yl + off, 4) * cores for off in offs]
+        shift = [log_norms[pl.ds(chip + c, 1), :] for chip in chips for c in range(cores)]
+        count = len(shift) * n
+        points = rows[...].reshape(count, d)
+        logits = products(table[...], columns(points)) - norms
         shares = jnp.exp(logits - jnp.concatenate(shift, axis=1)).astype(jnp.bfloat16)
-        product = jnp.dot(shares, pair, preferred_element_type=jnp.float32)
+        product = jnp.dot(shares, points, preferred_element_type=jnp.float32)
         wide = shares.astype(jnp.float32)
-        mass = sum(wide[:, i : i + 128] for i in range(0, cores * n, 128))
-        if at == 0:
+        mass = sum(wide[:, i : i + 128] for i in range(0, count, 128))
+        if rows is near:
             sums[...] = product
             masses[...] = mass
         else:

time: 69 us -> 68.8 us (level)
  no operation moved by 1% of the time
where the time goes in v8:
time: 68.8 us; the launch traced here: 68.5 us
  blocking collectives  37.3 us (54%)
  starting transfers between devices  11.6 us (17%)
  Pallas kernels  10.9 us (16%)
  waiting for transfers between devices  8.09 us (12%)
    all_to_all x1, blocking collectives, body(): parts = lax.all_to_all(parts, REDUCE, 0, 0, tiled=True)  26.3 us
    all_gather x1, blocking collectives, body(): near = lax.all_gather(points, 'co')  8.72 us
    all_to_all x1, waiting for transfers between devices, body(): every = lax.all_to_all(stats, (*CEN, *GATHER), 0, 0, tiled=True)  8.09 us
    all_to_all x1, starting transfers between devices, body(): every = lax.all_to_all(stats, (*CEN, *GATHER), 0, 0, tiled=True)  7.78 us
    pallas_call x1, Pallas kernels, first_pass(): pl.pallas_call(first_kernel, in_specs=[pl.BlockSpec(memory_space=pltpu.HB...  6.11 us
    ppermute x2, starting transfers between devices, moved(): return lax.ppermute(array, RING, pairs)  3.83 us
    pallas_call x1, Pallas kernels, second_pass(): pl.pallas_call(second_kernel, in_specs=[pl.BlockSpec(memory_space=pltpu.V...  3.68 us
    all_gather x1, blocking collectives, body(): sides = lax.all_gather(side, 'co')  2.26 us
  transfers between devices with their start and end apart: 3, of which 1 were waited for; matrix products, arithmetic and copies ran while one was open for 0% of the time, Pallas kernels for 9%

profile of v8, /device:TPU:1, one launch (start us, length us, event | category | flops | bytes accessed | tf_op | source)
XLA Modules:
  0.0 68.5 jit_solution(8293392178285125850)
XLA Ops:
  0.6 8.7 %all-gather = bf16[512,256]{1,0:T(8,128)(2,1)S(1)} all-gather(bf16[256,256]{1,0:T(8,128)(2,1)} %points.1), channel_id=2, replica_groups=mesh['yl'=4,'z'=8,'co'=2,'x'=4,'yh'=2] {'co'}, dimensions={0}, use_global_device_ids=true | all-gather | bytes 393216 | tf_op jit(solution)/shard_map/all_gather | solution.py:223
  9.4 1.9 %collective-permute-start = (bf16[2,256,256]{2,1,0:T(8,128)(2,1)S(1)}, bf16[2,256,256]{2,1,0:T(8,128)(2,1)S(1)}, u32[]{:S(2)}, u32[]{:S(2)}) collective-permute-start(bf16[2,256,256]{2,1,0:T(8,128)(2,1)S(1)} %bitcast.7), channel_id=1, source_target_pairs={{0,128},{8,393},{128,256},{136,8},{256,384},{264,136},{384,1},{392... | collective-permute-start | bytes 786440 | tf_op jit(solution)/shard_map/ppermute | solution.py:213
  11.3 1.9 %collective-permute-start.1 = (bf16[2,256,256]{2,1,0:T(8,128)(2,1)S(1)}, bf16[2,256,256]{2,1,0:T(8,128)(2,1)S(1)}, u32[]{:S(2)}, u32[]{:S(2)}) collective-permute-start(bf16[2,256,256]{2,1,0:T(8,128)(2,1)S(1)} %bitcast.8), channel_id=1, source_target_pairs={{0,256},{8,265},{128,384},{136,393},{256,1},{264,8},{384,129},{392... | collective-permute-start | bytes 786440 | tf_op jit(solution)/shard_map/ppermute | solution.py:213
  13.2 6.1 %first_pass.1 = (f32[64,2,256]{2,1,0:T(2,128)}, bf16[8,128,256]{2,1,0:T(8,128)(2,1)S(1)}) custom-call(bf16[8192,256]{1,0:T(8,128)(2,1)} %centroids.1, bf16[256,256]{1,0:T(8,128)(2,1)} %points.1), custom_call_target="tpu_custom_call" | custom-call | flops 1073741824 | bytes 4194304 | tf_op jit(solution)/shard_map/first_pass/pallas_call | solution.py:68
  19.3 7.8 %all-to-all-start = ((f32[64,2,256]{2,1,0:T(2,128)}), f32[64,2,256]{2,1,0:T(2,128)S(1)}, u32[]{:S(2)}, u32[]{:S(2)}) async-start(f32[64,2,256]{2,1,0:T(2,128)} %get-tuple-element.7), calls=%async_computation | async-start | bytes 262144 | tf_op jit(solution)/shard_map/all_to_all | solution.py:228
  27.1 0.0 collective-permute-done
  27.1 2.3 %all-gather.1 = bf16[4,256,256]{2,1,0:T(8,128)(2,1)S(1)} all-gather(bf16[2,256,256]{2,1,0:T(8,128)(2,1)S(1)} %collective-permute-done), channel_id=3, replica_groups=mesh['yl'=4,'z'=8,'co'=2,'x'=4,'yh'=2] {'co'}, dimensions={0}, use_global_device_ids=true | all-gather | bytes 786432 | tf_op jit(solution)/shard_map/all_gather | solution.py:227
  29.4 8.1 %all-to-all-done = f32[64,2,256]{2,1,0:T(2,128)S(1)} async-done(((f32[64,2,256]{2,1,0:T(2,128)}), f32[64,2,256]{2,1,0:T(2,128)S(1)}, u32[]{:S(2)}, u32[]{:S(2)}) %all-to-all-start) | async-done | bytes 131104 | tf_op jit(solution)/shard_map/all_to_all | solution.py:228
  37.5 0.0 collective-permute-done.1.far
  37.5 3.7 %second_pass.1 = (bf16[8,272,128]{2,1,0:T(8,128)(2,1)S(1)}, f32[1,256]{1,0:T(1,128)}) custom-call(f32[8,8,2,256]{3,2,1,0:T(2,128)S(1)} %bitcast.10, bf16[1024,256]{1,0:T(8,128)(2,1)S(1)} %bitcast.5, bf16[2,256,256]{2,1,0:T(8,128)(2,1)S(1)} %bitcast.9, bf16[2,2,256,256]{3,2,1,0:T(8,128)(2,1)S(1)} %bitcast.6, bf16[2,256,256]{2,1,0:T(8,128)(2,1)S(1)} %collective-permute-done.1.far), custom_call_target="tpu_custom_call" | custom-call | flops 2147483648 | bytes 1048576 | tf_op jit(solution)/shard_map/second_pass/pallas_call | solution.py:150
  41.1 26.3 %all_to_all.10.parts = bf16[8,272,128]{2,1,0:T(8,128)(2,1)S(1)} all-to-all(bf16[8,272,128]{2,1,0:T(8,128)(2,1)S(1)} %get-tuple-element.10), channel_id=1, replica_groups=mesh['yl'=4,'z'=8,'co'=2,'x'=4,'yh'=2] {'z'}, dimensions={0} | all-to-all | bytes 1114112 | tf_op jit(solution)/shard_map/all_to_all | solution.py:231
  67.4 1.1 %last_pass.1 = f32[128,256]{1,0:T(8,128)} custom-call(bf16[8,272,128]{2,1,0:T(8,128)(2,1)S(1)} %all_to_all.10.parts, bf16[8,128,256]{2,1,0:T(8,128)(2,1)S(1)} %get-tuple-element.8.table), custom_call_target="tpu_custom_call" | custom-call | tf_op jit(solution)/shard_map/last_pass/pallas_call | solution.py:191
Async XLA Ops:
  9.4 17.8 %collective-permute-start = (bf16[2,256,256]{2,1,0:T(8,128)(2,1)S(1)}, bf16[2,256,256]{2,1,0:T(8,128)(2,1)S(1)}, u32[]{:S(2)}, u32[]{:S(2)}) collective-permute-start(bf16[2,256,256]{2,1,0:T(8,128)(2,1)S(1)} %bitcast.7), channel_id=1, source_target_pairs={{0,128},{8,393},{128,256},{136,8},{256,384},{264,136},{384,1},{392... | collective-permute-start | bytes 786440 | tf_op jit(solution)/shard_map/ppermute | solution.py:213
  11.3 26.2 %collective-permute-start.1 = (bf16[2,256,256]{2,1,0:T(8,128)(2,1)S(1)}, bf16[2,256,256]{2,1,0:T(8,128)(2,1)S(1)}, u32[]{:S(2)}, u32[]{:S(2)}) collective-permute-start(bf16[2,256,256]{2,1,0:T(8,128)(2,1)S(1)} %bitcast.8), channel_id=1, source_target_pairs={{0,256},{8,265},{128,384},{136,393},{256,1},{264,8},{384,129},{392... | collective-permute-start | bytes 786440 | tf_op jit(solution)/shard_map/ppermute | solution.py:213
  19.3 18.1 %all-to-all-start = ((f32[64,2,256]{2,1,0:T(2,128)}), f32[64,2,256]{2,1,0:T(2,128)S(1)}, u32[]{:S(2)}, u32[]{:S(2)}) async-start(f32[64,2,256]{2,1,0:T(2,128)} %get-tuple-element.7), calls=%async_computation | async-start | bytes 262144 | tf_op jit(solution)/shard_map/all_to_all | solution.py:228

commit v9 on v8

--- a/solution.py
+++ b/solution.py
@@ -12,6 +12,7 @@
 REDUCE = "z"
 RING = ("yl", "co", "yh")
 MIB = 1 << 20
+ORDER = (7, 6, 5, 4, 3, 2, 1, 0)
 CHUNK = 2048
 inv_temp = 0.0625
 SPAN, FLOOR = 240.0, 120.0
@@ -58,7 +59,7 @@
     yl, co = (lax.axis_index(a) for a in GATHER)
     count, owned, _ = reduced.shape
     for z in range(count):
-        at = ((yl * count + z) * lax.axis_size("co") + co) * owned
+        at = ((yl * count + ORDER[z]) * lax.axis_size("co") + co) * owned
         reduced[z] = table[pl.ds(pl.multiple_of(at, owned), owned), :]
 
 
@@ -99,14 +100,14 @@
     for c in range(1, cen):
         total = total + stats[c, :, 1, :] * jnp.exp(stats[c, :, 0, :] - peak)
     log_norms[...] = peak + jnp.log(total)
-    own_norm[...] = log_norms[pl.ds(yl * 2 + co, 1), :]
+    own_norm[...] = log_norms[pl.ds(7 - yl * 2 - co, 1), :]
 
     norms = squares(table[...])
     cores, n, d = near.shape
     groups = ((near, (0,)), (sides, (3, 1)), (far, (2,)))
     for rows, offs in groups:
         chips = [lax.rem(yl + off, 4) * cores for off in offs]
-        shift = [log_norms[pl.ds(chip + c, 1), :] for chip in chips for c in range(cores)]
+        shift = [log_norms[pl.ds(7 - chip - c, 1), :] for chip in chips for c in range(cores)]
         count = len(shift) * n
         points = rows[...].reshape(count, d)
         logits = products(table[...], columns(points)) - norms
@@ -170,7 +171,8 @@
 
 def last_kernel(parts, table, updated):
     owned = updated.shape[0]
-    own = table[lax.axis_index(REDUCE)]
+    z = lax.axis_index(REDUCE)
+    own = table[sum(jnp.where(z == at, r, 0) for r, at in enumerate(ORDER))]
     sums = own.astype(jnp.float32)
     masses = jnp.ones((owned, owned), jnp.float32)
     for r in range(parts.shape[0]):
@@ -225,10 +227,13 @@
     stats, table = first_pass(points, centroids, cen * gathered, reduced, owned)
     side, _ = lax.optimization_barrier((side, stats))
     sides = lax.all_gather(side, "co")
-    every = lax.all_to_all(stats, (*CEN, *GATHER), 0, 0, tiled=True)
+    turned = [list(range(cen * gathered))[::-1]]
+    every = lax.all_to_all(
+        stats, (*CEN, *GATHER), 0, 0, tiled=True, axis_index_groups=turned
+    )
     every = every.reshape(cen, gathered, 2, n)
     parts, log_norm = second_pass(every, table, (near, sides, far))
-    parts = lax.all_to_all(parts, REDUCE, 0, 0, tiled=True)
+    parts = lax.all_to_all(parts, REDUCE, 0, 0, tiled=True, axis_index_groups=[list(ORDER)])
     return last_pass(parts, table), log_norm[0]
 
 

time: 68.8 us -> 66 us (0.959)
  waiting for transfers between devices: 8.09 us -> 4.24 us
  starting transfers between devices: 11.6 us -> 14 us
  blocking collectives: 37.3 us -> 35.9 us
    all_to_all x1, waiting for transfers between devices: 8.09 us -> 4.23 us  [body(): lax.all_to_all(stats, (*CEN, *GATHER), 0, 0, tiled=True, axis_index_group...]
    all_to_all x1, starting transfers between devices: 7.78 us -> 10.2 us  [body(): lax.all_to_all(stats, (*CEN, *GATHER), 0, 0, tiled=True, axis_index_group...]
    all_to_all x1, blocking collectives: 26.3 us -> 25 us  [body(): lax.all_to_all(parts, REDUCE, 0, 0, tiled=True, axis_index_groups=[list(O...]
where the time goes in v9:
time: 66 us; the launch traced here: 65.7 us
  blocking collectives  35.9 us (54%)
  starting transfers between devices  14 us (21%)
  Pallas kernels  10.9 us (17%)
  waiting for transfers between devices  4.24 us (6%)
  between operations  0.67 us (1%)
    all_to_all x1, blocking collectives, body(): lax.all_to_all(parts, REDUCE, 0, 0, tiled=True, axis_index_groups=[list(O...  25 us
    all_to_all x1, starting transfers between devices, body(): lax.all_to_all(stats, (*CEN, *GATHER), 0, 0, tiled=True, axis_index_group...  10.2 us
    all_gather x1, blocking collectives, body(): near = lax.all_gather(points, 'co')  8.72 us
    pallas_call x1, Pallas kernels, first_pass(): pl.pallas_call(first_kernel, in_specs=[pl.BlockSpec(memory_space=pltpu.HB...  6.11 us
    all_to_all x1, waiting for transfers between devices, body(): lax.all_to_all(stats, (*CEN, *GATHER), 0, 0, tiled=True, axis_index_group...  4.23 us
    ppermute x2, starting transfers between devices, moved(): return lax.ppermute(array, RING, pairs)  3.83 us
    pallas_call x1, Pallas kernels, second_pass(): pl.pallas_call(second_kernel, in_specs=[pl.BlockSpec(memory_space=pltpu.V...  3.69 us
    all_gather x1, blocking collectives, body(): sides = lax.all_gather(side, 'co')  2.24 us
  transfers between devices with their start and end apart: 3, of which 1 were waited for; matrix products, arithmetic and copies ran while one was open for 0% of the time, Pallas kernels for 9%

profile of v9, /device:TPU:1, one launch (start us, length us, event | category | flops | bytes accessed | tf_op | source)
XLA Modules:
  0.0 65.7 jit_solution(2979623355936387319)
XLA Ops:
  0.6 8.7 %all-gather = bf16[512,256]{1,0:T(8,128)(2,1)S(1)} all-gather(bf16[256,256]{1,0:T(8,128)(2,1)} %points.1), channel_id=2, replica_groups=mesh['yl'=4,'z'=8,'co'=2,'x'=4,'yh'=2] {'co'}, dimensions={0}, use_global_device_ids=true | all-gather | bytes 393216 | tf_op jit(solution)/shard_map/all_gather | solution.py:225
  9.4 1.9 %collective-permute-start = (bf16[2,256,256]{2,1,0:T(8,128)(2,1)S(1)}, bf16[2,256,256]{2,1,0:T(8,128)(2,1)S(1)}, u32[]{:S(2)}, u32[]{:S(2)}) collective-permute-start(bf16[2,256,256]{2,1,0:T(8,128)(2,1)S(1)} %bitcast.7), channel_id=1, source_target_pairs={{0,128},{8,393},{128,256},{136,8},{256,384},{264,136},{384,1},{392... | collective-permute-start | bytes 786440 | tf_op jit(solution)/shard_map/ppermute | solution.py:215
  11.3 1.9 %collective-permute-start.1 = (bf16[2,256,256]{2,1,0:T(8,128)(2,1)S(1)}, bf16[2,256,256]{2,1,0:T(8,128)(2,1)S(1)}, u32[]{:S(2)}, u32[]{:S(2)}) collective-permute-start(bf16[2,256,256]{2,1,0:T(8,128)(2,1)S(1)} %bitcast.8), channel_id=1, source_target_pairs={{0,256},{8,265},{128,384},{136,393},{256,1},{264,8},{384,129},{392... | collective-permute-start | bytes 786440 | tf_op jit(solution)/shard_map/ppermute | solution.py:215
  13.2 6.1 %first_pass.1 = (f32[64,2,256]{2,1,0:T(2,128)}, bf16[8,128,256]{2,1,0:T(8,128)(2,1)S(1)}) custom-call(bf16[8192,256]{1,0:T(8,128)(2,1)} %centroids.1, bf16[256,256]{1,0:T(8,128)(2,1)} %points.1), custom_call_target="tpu_custom_call" | custom-call | flops 1073741824 | bytes 4194304 | tf_op jit(solution)/shard_map/first_pass/pallas_call | solution.py:69
  19.3 10.2 %all-to-all-start = ((f32[64,2,256]{2,1,0:T(2,128)}), f32[64,2,256]{2,1,0:T(2,128)S(1)}, u32[]{:S(2)}, u32[]{:S(2)}) async-start(f32[64,2,256]{2,1,0:T(2,128)} %get-tuple-element.7), calls=%async_computation | async-start | bytes 262144 | tf_op jit(solution)/shard_map/all_to_all | solution.py:231
  29.5 0.0 collective-permute-done
  29.5 2.2 %all-gather.1 = bf16[4,256,256]{2,1,0:T(8,128)(2,1)S(1)} all-gather(bf16[2,256,256]{2,1,0:T(8,128)(2,1)S(1)} %collective-permute-done), channel_id=3, replica_groups=mesh['yl'=4,'z'=8,'co'=2,'x'=4,'yh'=2] {'co'}, dimensions={0}, use_global_device_ids=true | all-gather | bytes 786432 | tf_op jit(solution)/shard_map/all_gather | solution.py:229
  31.7 4.2 %all-to-all-done = f32[64,2,256]{2,1,0:T(2,128)S(1)} async-done(((f32[64,2,256]{2,1,0:T(2,128)}), f32[64,2,256]{2,1,0:T(2,128)S(1)}, u32[]{:S(2)}, u32[]{:S(2)}) %all-to-all-start) | async-done | bytes 131104 | tf_op jit(solution)/shard_map/all_to_all | solution.py:231
  36.0 0.0 collective-permute-done.1.far
  36.0 3.7 %second_pass.1 = (bf16[8,272,128]{2,1,0:T(8,128)(2,1)S(1)}, f32[1,256]{1,0:T(1,128)}) custom-call(f32[8,8,2,256]{3,2,1,0:T(2,128)S(1)} %bitcast.10, bf16[1024,256]{1,0:T(8,128)(2,1)S(1)} %bitcast.5, bf16[2,256,256]{2,1,0:T(8,128)(2,1)S(1)} %bitcast.9, bf16[2,2,256,256]{3,2,1,0:T(8,128)(2,1)S(1)} %bitcast.6, bf16[2,256,256]{2,1,0:T(8,128)(2,1)S(1)} %collective-permute-done.1.far), custom_call_target="tpu_custom_call" | custom-call | flops 2147483648 | bytes 1048576 | tf_op jit(solution)/shard_map/second_pass/pallas_call | solution.py:151
  39.7 25.0 %all_to_all.10.parts = bf16[8,272,128]{2,1,0:T(8,128)(2,1)S(1)} all-to-all(bf16[8,272,128]{2,1,0:T(8,128)(2,1)S(1)} %get-tuple-element.10), channel_id=1, replica_groups={{112,96,80,64,48,32,16,0},{113,97,81,65,49,33,17,1},{114,98,82,66,50,34..., dimensions={0} | all-to-all | bytes 1114112 | tf_op jit(solution)/shard_map/all_to_all | solution.py:236
  64.6 1.1 %last_pass.1 = f32[128,256]{1,0:T(8,128)} custom-call(bf16[8,272,128]{2,1,0:T(8,128)(2,1)S(1)} %all_to_all.10.parts, bf16[8,128,256]{2,1,0:T(8,128)(2,1)S(1)} %get-tuple-element.8.table), custom_call_target="tpu_custom_call" | custom-call | tf_op jit(solution)/shard_map/last_pass/pallas_call | solution.py:193
Async XLA Ops:
  9.4 20.1 %collective-permute-start = (bf16[2,256,256]{2,1,0:T(8,128)(2,1)S(1)}, bf16[2,256,256]{2,1,0:T(8,128)(2,1)S(1)}, u32[]{:S(2)}, u32[]{:S(2)}) collective-permute-start(bf16[2,256,256]{2,1,0:T(8,128)(2,1)S(1)} %bitcast.7), channel_id=1, source_target_pairs={{0,128},{8,393},{128,256},{136,8},{256,384},{264,136},{384,1},{392... | collective-permute-start | bytes 786440 | tf_op jit(solution)/shard_map/ppermute | solution.py:215
  11.3 24.7 %collective-permute-start.1 = (bf16[2,256,256]{2,1,0:T(8,128)(2,1)S(1)}, bf16[2,256,256]{2,1,0:T(8,128)(2,1)S(1)}, u32[]{:S(2)}, u32[]{:S(2)}) collective-permute-start(bf16[2,256,256]{2,1,0:T(8,128)(2,1)S(1)} %bitcast.8), channel_id=1, source_target_pairs={{0,256},{8,265},{128,384},{136,393},{256,1},{264,8},{384,129},{392... | collective-permute-start | bytes 786440 | tf_op jit(solution)/shard_map/ppermute | solution.py:215
  19.3 16.7 %all-to-all-start = ((f32[64,2,256]{2,1,0:T(2,128)}), f32[64,2,256]{2,1,0:T(2,128)S(1)}, u32[]{:S(2)}, u32[]{:S(2)}) async-start(f32[64,2,256]{2,1,0:T(2,128)} %get-tuple-element.7), calls=%async_computation | async-start | bytes 262144 | tf_op jit(solution)/shard_map/all_to_all | solution.py:231

commit v10 on v9

--- a/solution.py
+++ b/solution.py
@@ -12,7 +12,7 @@
 REDUCE = "z"
 RING = ("yl", "co", "yh")
 MIB = 1 << 20
-ORDER = (7, 6, 5, 4, 3, 2, 1, 0)
+ORDER = (7, 3, 6, 2, 5, 1, 4, 0)
 CHUNK = 2048
 inv_temp = 0.0625
 SPAN, FLOOR = 240.0, 120.0

time: 66 us -> 65.6 us (level)
  blocking collectives: 35.9 us -> 35.2 us
    all_to_all x1, blocking collectives: 25 us -> 24.2 us  [body(): lax.all_to_all(parts, REDUCE, 0, 0, tiled=True, axis_index_groups=[list(O...]
where the time goes in v10:
time: 65.6 us; the launch traced here: 64.9 us
  blocking collectives  35.2 us (54%)
  starting transfers between devices  14 us (21%)
  Pallas kernels  10.9 us (17%)
  waiting for transfers between devices  4.24 us (6%)
  between operations  0.67 us (1%)
    all_to_all x1, blocking collectives, body(): lax.all_to_all(parts, REDUCE, 0, 0, tiled=True, axis_index_groups=[list(O...  24.2 us
    all_to_all x1, starting transfers between devices, body(): lax.all_to_all(stats, (*CEN, *GATHER), 0, 0, tiled=True, axis_index_group...  10.2 us
    all_gather x1, blocking collectives, body(): near = lax.all_gather(points, 'co')  8.72 us
    pallas_call x1, Pallas kernels, first_pass(): pl.pallas_call(first_kernel, in_specs=[pl.BlockSpec(memory_space=pltpu.HB...  6.11 us
    all_to_all x1, waiting for transfers between devices, body(): lax.all_to_all(stats, (*CEN, *GATHER), 0, 0, tiled=True, axis_index_group...  4.23 us
    ppermute x2, starting transfers between devices, moved(): return lax.ppermute(array, RING, pairs)  3.83 us
    pallas_call x1, Pallas kernels, second_pass(): pl.pallas_call(second_kernel, in_specs=[pl.BlockSpec(memory_space=pltpu.V...  3.69 us
    all_gather x1, blocking collectives, body(): sides = lax.all_gather(side, 'co')  2.24 us
  transfers between devices with their start and end apart: 3, of which 1 were waited for; matrix products, arithmetic and copies ran while one was open for 0% of the time, Pallas kernels for 9%

profile of v10, /device:TPU:1, one launch (start us, length us, event | category | flops | bytes accessed | tf_op | source)
XLA Modules:
  0.0 64.9 jit_solution(15458323558848161882)
XLA Ops:
  0.6 8.7 %all-gather = bf16[512,256]{1,0:T(8,128)(2,1)S(1)} all-gather(bf16[256,256]{1,0:T(8,128)(2,1)} %points.1), channel_id=2, replica_groups=mesh['yl'=4,'z'=8,'co'=2,'x'=4,'yh'=2] {'co'}, dimensions={0}, use_global_device_ids=true | all-gather | bytes 393216 | tf_op jit(solution)/shard_map/all_gather | solution.py:225
  9.4 1.9 %collective-permute-start = (bf16[2,256,256]{2,1,0:T(8,128)(2,1)S(1)}, bf16[2,256,256]{2,1,0:T(8,128)(2,1)S(1)}, u32[]{:S(2)}, u32[]{:S(2)}) collective-permute-start(bf16[2,256,256]{2,1,0:T(8,128)(2,1)S(1)} %bitcast.7), channel_id=1, source_target_pairs={{0,128},{8,393},{128,256},{136,8},{256,384},{264,136},{384,1},{392... | collective-permute-start | bytes 786440 | tf_op jit(solution)/shard_map/ppermute | solution.py:215
  11.3 1.9 %collective-permute-start.1 = (bf16[2,256,256]{2,1,0:T(8,128)(2,1)S(1)}, bf16[2,256,256]{2,1,0:T(8,128)(2,1)S(1)}, u32[]{:S(2)}, u32[]{:S(2)}) collective-permute-start(bf16[2,256,256]{2,1,0:T(8,128)(2,1)S(1)} %bitcast.8), channel_id=1, source_target_pairs={{0,256},{8,265},{128,384},{136,393},{256,1},{264,8},{384,129},{392... | collective-permute-start | bytes 786440 | tf_op jit(solution)/shard_map/ppermute | solution.py:215
  13.2 6.1 %first_pass.1 = (f32[64,2,256]{2,1,0:T(2,128)}, bf16[8,128,256]{2,1,0:T(8,128)(2,1)S(1)}) custom-call(bf16[8192,256]{1,0:T(8,128)(2,1)} %centroids.1, bf16[256,256]{1,0:T(8,128)(2,1)} %points.1), custom_call_target="tpu_custom_call" | custom-call | flops 1073741824 | bytes 4194304 | tf_op jit(solution)/shard_map/first_pass/pallas_call | solution.py:69
  19.3 10.2 %all-to-all-start = ((f32[64,2,256]{2,1,0:T(2,128)}), f32[64,2,256]{2,1,0:T(2,128)S(1)}, u32[]{:S(2)}, u32[]{:S(2)}) async-start(f32[64,2,256]{2,1,0:T(2,128)} %get-tuple-element.7), calls=%async_computation | async-start | bytes 262144 | tf_op jit(solution)/shard_map/all_to_all | solution.py:231
  29.5 0.0 collective-permute-done
  29.5 2.2 %all-gather.1 = bf16[4,256,256]{2,1,0:T(8,128)(2,1)S(1)} all-gather(bf16[2,256,256]{2,1,0:T(8,128)(2,1)S(1)} %collective-permute-done), channel_id=3, replica_groups=mesh['yl'=4,'z'=8,'co'=2,'x'=4,'yh'=2] {'co'}, dimensions={0}, use_global_device_ids=true | all-gather | bytes 786432 | tf_op jit(solution)/shard_map/all_gather | solution.py:229
  31.7 4.2 %all-to-all-done = f32[64,2,256]{2,1,0:T(2,128)S(1)} async-done(((f32[64,2,256]{2,1,0:T(2,128)}), f32[64,2,256]{2,1,0:T(2,128)S(1)}, u32[]{:S(2)}, u32[]{:S(2)}) %all-to-all-start) | async-done | bytes 131104 | tf_op jit(solution)/shard_map/all_to_all | solution.py:231
  36.0 0.0 collective-permute-done.1.far
  36.0 3.7 %second_pass.1 = (bf16[8,272,128]{2,1,0:T(8,128)(2,1)S(1)}, f32[1,256]{1,0:T(1,128)}) custom-call(f32[8,8,2,256]{3,2,1,0:T(2,128)S(1)} %bitcast.10, bf16[1024,256]{1,0:T(8,128)(2,1)S(1)} %bitcast.5, bf16[2,256,256]{2,1,0:T(8,128)(2,1)S(1)} %bitcast.9, bf16[2,2,256,256]{3,2,1,0:T(8,128)(2,1)S(1)} %bitcast.6, bf16[2,256,256]{2,1,0:T(8,128)(2,1)S(1)} %collective-permute-done.1.far), custom_call_target="tpu_custom_call" | custom-call | flops 2147483648 | bytes 1048576 | tf_op jit(solution)/shard_map/second_pass/pallas_call | solution.py:151
  39.7 24.2 %all_to_all.10.parts = bf16[8,272,128]{2,1,0:T(8,128)(2,1)S(1)} all-to-all(bf16[8,272,128]{2,1,0:T(8,128)(2,1)S(1)} %get-tuple-element.10), channel_id=1, replica_groups={{112,48,96,32,80,16,64,0},{113,49,97,33,81,17,65,1},{114,50,98,34,82,18..., dimensions={0} | all-to-all | bytes 1114112 | tf_op jit(solution)/shard_map/all_to_all | solution.py:236
  63.9 1.1 %last_pass.1 = f32[128,256]{1,0:T(8,128)} custom-call(bf16[8,272,128]{2,1,0:T(8,128)(2,1)S(1)} %all_to_all.10.parts, bf16[8,128,256]{2,1,0:T(8,128)(2,1)S(1)} %get-tuple-element.8.table), custom_call_target="tpu_custom_call" | custom-call | tf_op jit(solution)/shard_map/last_pass/pallas_call | solution.py:193
Async XLA Ops:
  9.4 20.1 %collective-permute-start = (bf16[2,256,256]{2,1,0:T(8,128)(2,1)S(1)}, bf16[2,256,256]{2,1,0:T(8,128)(2,1)S(1)}, u32[]{:S(2)}, u32[]{:S(2)}) collective-permute-start(bf16[2,256,256]{2,1,0:T(8,128)(2,1)S(1)} %bitcast.7), channel_id=1, source_target_pairs={{0,128},{8,393},{128,256},{136,8},{256,384},{264,136},{384,1},{392... | collective-permute-start | bytes 786440 | tf_op jit(solution)/shard_map/ppermute | solution.py:215
  11.3 24.7 %collective-permute-start.1 = (bf16[2,256,256]{2,1,0:T(8,128)(2,1)S(1)}, bf16[2,256,256]{2,1,0:T(8,128)(2,1)S(1)}, u32[]{:S(2)}, u32[]{:S(2)}) collective-permute-start(bf16[2,256,256]{2,1,0:T(8,128)(2,1)S(1)} %bitcast.8), channel_id=1, source_target_pairs={{0,256},{8,265},{128,384},{136,393},{256,1},{264,8},{384,129},{392... | collective-permute-start | bytes 786440 | tf_op jit(solution)/shard_map/ppermute | solution.py:215
  19.3 16.7 %all-to-all-start = ((f32[64,2,256]{2,1,0:T(2,128)}), f32[64,2,256]{2,1,0:T(2,128)S(1)}, u32[]{:S(2)}, u32[]{:S(2)}) async-start(f32[64,2,256]{2,1,0:T(2,128)} %get-tuple-element.7), calls=%async_computation | async-start | bytes 262144 | tf_op jit(solution)/shard_map/all_to_all | solution.py:231
